TPU v7x, 32 devices: a whole 2x2x4 slice. The times are simulated.
32 devices in a mesh: groups: 2 (over x), strip: 16 (over z, y, core).
Axes of the slice: x: 2, y: 2, z: 4, core: 2. Of those that a mesh axis runs over, the one named last changes fastest.
Arguments:
- features: bfloat16 [256, 32, 1024], P(('groups', 'strip')), parts along dimension 0, may hold values from -9 to 9
- valid_rows: int32 [32], P(('groups', 'strip')), parts along dimension 0, may hold values from 1 to 8, as said below
- left_views: int32 [4, 4], P('groups'), parts along dimension 0, may hold values from 0 to 3, each once within a row
- right_step: int32 [4, 4], P('groups'), parts along dimension 0, may hold values from 1 to 3
- offset_tile: int32 [4, 4], P('groups'), parts along dimension 0, may hold values from 0 to 3
Outputs:
- disparity: float32 [2, 256, 1024], P(None, ('groups', 'strip')), parts along dimension 1
There are 2 independent parts, one for each index of `groups`. A program takes and returns all parts, laid end to end along the dimension named above; each array names one. Nothing has to cross between parts.
Inputs may be any that keep to these rules, and one draw needn't show every extreme that they name: `valid_rows`: at least one strip is full in every draw.
All inputs are finite; a program needn't handle non-finite values.
Results may differ from a plain program's by a relative error of at most 0.00075.
Values may be sent and summed in bfloat16 or wider, within the bound.
No kernel may reach another device: no remote copies, remote signals or barrier semaphores. Data moves between devices by JAX's collectives and lax.ppermute only.
A program may use at most 128 MiB of HBM per device.

v0:
```python
import jax
import jax.numpy as jnp
from jax import lax
from jax.sharding import PartitionSpec as P

LEVELS = 256
BX = 128
TILES = 4
VIEWS = 4
ROUNDS = 2


score_scale = 0.35


def from_behind(value, axis, steps):
    count = lax.axis_size(axis)
    pairs = [(source, (source + steps) % count) for source in range(count)]
    return lax.ppermute(value, axis, pairs)


def with_halo(array, sides, width):
    for axis, dim in sides:
        peers, length = (lax.axis_size(axis), array.shape[dim])
        up = [(i, (i + 1) % peers) for i in range(peers)]
        down = [(j, i) for i, j in up]
        last = lax.slice_in_dim(array, length - width, length, axis=dim)
        initial = lax.slice_in_dim(array, 0, width, axis=dim)
        before = lax.ppermute(last, axis, up)
        after = lax.ppermute(initial, axis, down)
        array = jnp.concatenate([before, array, after], axis=dim)
    return array


def right_windows(right_strip, tile_index):
    height, channels, columns = right_strip.shape
    block_count = columns // BX
    spans = right_strip.reshape(height, channels, block_count, BX)
    leading = jnp.zeros((height, channels, LEVELS // BX + TILES - 1, BX), right_strip.dtype)
    padded = jnp.concatenate([leading, spans], axis=2)
    pieces = []
    for window_part in range((BX + LEVELS) // BX):
        start = TILES - 1 - tile_index + window_part
        pieces.append(lax.dynamic_slice_in_dim(padded, start, block_count, 2))
    return jnp.concatenate(pieces, axis=3)


def block_scores(left_strip, right_strip, tile_index):
    height, channels, columns = left_strip.shape
    left_blocks = left_strip.reshape(height, channels, columns // BX, BX)
    windows = right_windows(right_strip, tile_index)
    return (
        jnp.einsum("ycnx,ycnj->ynxj", left_blocks, windows, preferred_element_type=jnp.float32)
        * score_scale
    )


def regress(padded, tile_index):
    aggregated = 0.25 * padded[:-2] + 0.5 * padded[1:-1] + 0.25 * padded[2:]
    columns = lax.broadcasted_iota(jnp.int32, (BX, BX + LEVELS), 0)
    window_cols = lax.broadcasted_iota(jnp.int32, (BX, BX + LEVELS), 1)
    levels_at = columns + LEVELS - window_cols
    in_band = (levels_at >= 0) & (levels_at < LEVELS)
    logits = jnp.where(in_band, aggregated, jnp.float32(-1e30))
    largest = jnp.max(logits, axis=-1, keepdims=True)
    weights = jnp.where(in_band, jnp.exp(logits - largest), jnp.float32(0.0))
    values = (tile_index * BX + levels_at).astype(jnp.float32)
    return jnp.sum(weights * values, axis=-1) / jnp.sum(weights, axis=-1)


def per_device(features, valid_rows, left_views, right_step, offset_tile):
    row_count = features.shape[0]
    col_count = features.shape[2]
    devices = lax.axis_size("strip")
    per_view = devices // VIEWS
    row_ids = lax.broadcasted_iota(jnp.int32, (row_count, 1, 1), 0)
    masked = jnp.where(row_ids >= row_count - valid_rows[0], features, jnp.zeros_like(features))
    pieces = [masked]
    for offset in range(1, VIEWS):
        pieces.append(from_behind(masked, "strip", devices - offset * per_view))
    stacked = jnp.stack(pieces, 0)
    device_index = lax.axis_index("strip")
    view_place = (device_index - per_view // 2) % devices
    own_view = view_place // per_view
    position = view_place % per_view
    top_keep = (position > 0).astype(jnp.float32).reshape(1)
    bottom_keep = (position < per_view - 1).astype(jnp.float32).reshape(1)
    rim_keep = jnp.concatenate([top_keep, jnp.ones((row_count,), jnp.float32), bottom_keep])
    outputs = []
    for round_index in range(ROUNDS):
        left_view = left_views[round_index, own_view]
        right_view = (left_view + right_step[round_index, own_view]) % VIEWS
        tile_index = offset_tile[round_index, own_view]
        left_strip = lax.dynamic_index_in_dim(
            stacked, (left_view - own_view) % VIEWS, 0, keepdims=False
        )
        right_strip = lax.dynamic_index_in_dim(
            stacked, (right_view - own_view) % VIEWS, 0, keepdims=False
        )
        widened = with_halo(jnp.stack([left_strip, right_strip], 1), (("strip", 0),), 1)
        wide_left = widened[:, 0] * rim_keep.astype(jnp.bfloat16)[:, None, None]
        padded = block_scores(wide_left, widened[:, 1], tile_index)
        result = regress(padded, tile_index)
        outputs.append(result.reshape(row_count, col_count))
    return jnp.stack(outputs, 0)


def solution(mesh):
    return jax.shard_map(
        per_device,
        mesh=mesh,
        in_specs=(
            P(("groups", "strip"), None, None),
            P(("groups", "strip")),
            P("groups", None),
            P("groups", None),
            P("groups", None),
        ),
        out_specs=P(None, ("groups", "strip"), None),
        check_vma=False,
    )
```

profile of v0, /device:TPU:0, one launch (start us, length us, event | category | flops | bytes accessed | tf_op | source)
XLA Modules:
  0.0 148.2 jit_solution(16002352031332113204)
XLA Ops:
  0.7 1.1 broadcast_select_fusion
  1.8 5.1 %collective-permute-start = (bf16[8,32,1024]{2,1,0:T(8,128)(2,1)S(1)}, bf16[8,32,1024]{2,1,0:T(8,128)(2,1)S(1)}, u32[]{:S(2)}, u32[]{:S(2)}) collective-permute-start(bf16[8,32,1024]{2,1,0:T(8,128)(2,1)S(1)} %broadcast_select_fusion), channel_id=1, source_target_pairs={{0,12},{1,13},{2,14},{3,15},{4,0},{5,1},{6,2},{7,3},{8,4},{9,5},{1... | collective-permute-start | bytes 1572872 | tf_op jit(solution)/shard_map/ppermute | solution.py:19
  6.9 1.0 collective-permute-start.2
  8.1 1.4 constant_dynamic-slice_fusion.2
  9.5 1.4 constant_dynamic-slice_fusion
  16.0 1.1 fusion.31
  17.1 2.1 %collective-permute-done = bf16[8,32,1024]{2,1,0:T(8,128)(2,1)S(1)} collective-permute-done((bf16[8,32,1024]{2,1,0:T(8,128)(2,1)S(1)}, bf16[8,32,1024]{2,1,0:T(8,128)(2,1)S(1)}, u32[]{:S(2)}, u32[]{:S(2)}) %collective-permute-start) | collective-permute-done | bytes 524320 | tf_op jit(solution)/shard_map/ppermute | solution.py:19
  19.3 32.4 %collective-permute-done.1 = bf16[8,32,1024]{2,1,0:T(8,128)(2,1)S(1)} collective-permute-done((bf16[8,32,1024]{2,1,0:T(8,128)(2,1)S(1)}, bf16[8,32,1024]{2,1,0:T(8,128)(2,1)S(1)}, u32[]{:S(2)}, u32[]{:S(2)}) %collective-permute-start.1) | collective-permute-done | bytes 524320 | tf_op jit(solution)/shard_map/ppermute | solution.py:19
  51.7 0.3 pad_maximum_fusion
  52.0 0.2 dynamic-slice_bitcast_fusion.3
  52.3 4.4 %collective-permute-start.6 = (bf16[1,2,32,1024]{3,2,0,1:T(8,128)(2,1)S(1)}, bf16[1,2,32,1024]{3,2,0,1:T(8,128)(2,1)S(1)}, u32[]{:S(2)}, u32[]{:S(2)}) collective-permute-start(bf16[1,2,32,1024]{3,2,0,1:T(8,128)(2,1)S(1)} %get-tuple-element.20), channel_id=1, source_target_pairs={{1,0},{2,1},{3,2},{4,3},{5,4},{6,5},{7,6},{8,7},{9,8},{10,9},{11,1... | collective-permute-start | bytes 393224 | tf_op jit(solution)/shard_map/ppermute | solution.py:30
  64.4 4.4 %collective-permute-start.4 = (bf16[1,2,32,1024]{3,2,0,1:T(8,128)(2,1)S(1)}, bf16[1,2,32,1024]{3,2,0,1:T(8,128)(2,1)S(1)}, u32[]{:S(2)}, u32[]{:S(2)}) collective-permute-start(bf16[1,2,32,1024]{3,2,0,1:T(8,128)(2,1)S(1)} %get-tuple-element.18), channel_id=1, source_target_pairs={{1,0},{2,1},{3,2},{4,3},{5,4},{6,5},{7,6},{8,7},{9,8},{10,9},{11,1... | collective-permute-start | bytes 393224 | tf_op jit(solution)/shard_map/ppermute | solution.py:30
  68.9 0.2 pad_maximum_fusion.2
  69.6 1.9 %collective-permute-done.3 = bf16[1,2,32,1024]{3,2,0,1:T(8,128)(2,1)S(1)} collective-permute-done((bf16[1,2,32,1024]{3,2,0,1:T(8,128)(2,1)S(1)}, bf16[1,2,32,1024]{3,2,0,1:T(8,128)(2,1)S(1)}, u32[]{:S(2)}, u32[]{:S(2)}) %collective-permute-start.3) | collective-permute-done | bytes 131104 | tf_op jit(solution)/shard_map/ppermute | solution.py:29
  71.5 0.2 pad_maximum_fusion.1
  72.2 0.2 bitcast_multiply_fusion.1
  72.4 0.5 pad_dynamic-slice_fusion.2
  72.9 6.8 %convolution_multiply_fusion = f32[10,8,128,384]{3,2,1,0:T(8,128)} fusion(bf16[10,32,8,128]{3,1,2,0:T(8,128)(2,1)S(1)} %get-tuple-element.26, bf16[10,32,8,128]{3,1,2,0:T(8,128)(2,1)S(1)} %get-tuple-element.25, bf16[10,32,8,128]{3,1,2,0:T(8,128)(2,1)S(1)} %get-tuple-element.24, bf16[10,32,8,128]{3,2,1,0:T(8,128)(2,1)S(1)} %get-tuple-element.38), kind=kOutput, calls=%fused_computation.18 | convolution fusion | flops 261488640 | bytes 18350080 | tf_op jit(solution)/shard_map/ycnx,ycnj->ynxj/dot_general | solution.py:53
  79.7 0.5 pad_dynamic-slice_fusion.5
  80.1 6.8 %convolution_multiply_fusion.1 = f32[10,8,128,384]{3,2,1,0:T(8,128)} fusion(bf16[10,32,8,128]{3,1,2,0:T(8,128)(2,1)S(1)} %get-tuple-element.23, bf16[10,32,8,128]{3,1,2,0:T(8,128)(2,1)S(1)} %get-tuple-element.22, bf16[10,32,8,128]{3,1,2,0:T(8,128)(2,1)S(1)} %get-tuple-element.21, bf16[10,32,8,128]{3,2,1,0:T(8,128)(2,1)S(1)} %get-tuple-element.37), kind=kOutput, calls=%fused_computation.19 | convolution fusion | flops 261488640 | bytes 18350080 | tf_op jit(solution)/shard_map/ycnx,ycnj->ynxj/dot_general | solution.py:53
  86.9 35.0 %fusion.6 = (f32[8,8,128,384]{3,2,1,0:T(8,128)}, f32[8,8,128,384]{3,2,1,0:T(8,128)}) fusion(f32[10,8,128,384]{3,2,1,0:T(8,128)} %convolution_multiply_fusion.1, pred[128,384]{1,0:T(8,128)(4,1)S(1)} %fusion.22, f32[10,8,128,384]{3,2,1,0:T(8,128)} %convolution_multiply_fusion), kind=kLoop, calls=%fused_computation.10 | loop fusion | flops 37748736 | bytes 100712448 | tf_op jit(solution)/shard_map/jit(_where)/select_n | solution.py:64
  121.9 12.8 %fusion.25 = (f32[8,8,128]{2,1,0:T(8,128)S(1)}, f32[8,8,128]{2,1,0:T(8,128)S(1)}) fusion(f32[128,384]{1,0:T(8,128)S(1)} %get-tuple-element.35, f32[8,8,128,384]{3,2,1,0:T(8,128)} %get-tuple-element.27, pred[128,384]{1,0:T(8,128)(4,1)S(1)} %fusion.22), kind=kOutput, calls=%fused_computation.70 | output fusion | flops 15720831 | bytes 12894208 | tf_op jit(solution)/shard_map/sub | solution.py:66
  134.7 12.8 %fusion.26 = (f32[8,8,128]{2,1,0:T(8,128)S(1)}, f32[8,8,128]{2,1,0:T(8,128)S(1)}) fusion(f32[128,384]{1,0:T(8,128)S(1)} %get-tuple-element.36, f32[8,8,128,384]{3,2,1,0:T(8,128)} %get-tuple-element.28, pred[128,384]{1,0:T(8,128)(4,1)S(1)} %fusion.22), kind=kOutput, calls=%fused_computation.71 | output fusion | flops 15720831 | bytes 12894208 | tf_op jit(solution)/shard_map/sub | solution.py:66
  147.6 0.6 pad_maximum_fusion.7
  (27 shorter events, 1.5 us)
Async XLA Ops:
  1.8 17.5 %collective-permute-start = (bf16[8,32,1024]{2,1,0:T(8,128)(2,1)S(1)}, bf16[8,32,1024]{2,1,0:T(8,128)(2,1)S(1)}, u32[]{:S(2)}, u32[]{:S(2)}) collective-permute-start(bf16[8,32,1024]{2,1,0:T(8,128)(2,1)S(1)} %broadcast_select_fusion), channel_id=1, source_target_pairs={{0,12},{1,13},{2,14},{3,15},{4,0},{5,1},{6,2},{7,3},{8,4},{9,5},{1... | collective-permute-start | bytes 1572872 | tf_op jit(solution)/shard_map/ppermute | solution.py:19
  6.9 44.8 %collective-permute-start.1 = (bf16[8,32,1024]{2,1,0:T(8,128)(2,1)S(1)}, bf16[8,32,1024]{2,1,0:T(8,128)(2,1)S(1)}, u32[]{:S(2)}, u32[]{:S(2)}) collective-permute-start(bf16[8,32,1024]{2,1,0:T(8,128)(2,1)S(1)} %broadcast_select_fusion), channel_id=1, source_target_pairs={{0,8},{1,9},{2,10},{3,11},{4,12},{5,13},{6,14},{7,15},{8,0},{9,1},... | collective-permute-start | bytes 1572872 | tf_op jit(solution)/shard_map/ppermute | solution.py:19
  6.9 44.8 %collective-permute-start.2 = (bf16[8,32,1024]{2,1,0:T(8,128)(2,1)S(1)}, bf16[8,32,1024]{2,1,0:T(8,128)(2,1)S(1)}, u32[]{:S(2)}, u32[]{:S(2)}) collective-permute-start(bf16[8,32,1024]{2,1,0:T(8,128)(2,1)S(1)} %broadcast_select_fusion), channel_id=1, source_target_pairs={{0,4},{1,5},{2,6},{3,7},{4,8},{5,9},{6,10},{7,11},{8,12},{9,13},{1... | collective-permute-start | bytes 1572872 | tf_op jit(solution)/shard_map/ppermute | solution.py:19
  52.2 16.7 %collective-permute-start.5 = (bf16[1,2,32,1024]{3,2,0,1:T(8,128)(2,1)S(1)}, bf16[1,2,32,1024]{3,2,0,1:T(8,128)(2,1)S(1)}, u32[]{:S(2)}, u32[]{:S(2)}) collective-permute-start(bf16[1,2,32,1024]{3,2,0,1:T(8,128)(2,1)S(1)} %get-tuple-element.19), channel_id=1, source_target_pairs={{0,1},{1,2},{2,3},{3,4},{4,5},{5,6},{6,7},{7,8},{8,9},{9,10},{10,1... | collective-permute-start | bytes 393224 | tf_op jit(solution)/shard_map/ppermute | solution.py:29
  52.3 16.6 %collective-permute-start.6 = (bf16[1,2,32,1024]{3,2,0,1:T(8,128)(2,1)S(1)}, bf16[1,2,32,1024]{3,2,0,1:T(8,128)(2,1)S(1)}, u32[]{:S(2)}, u32[]{:S(2)}) collective-permute-start(bf16[1,2,32,1024]{3,2,0,1:T(8,128)(2,1)S(1)} %get-tuple-element.20), channel_id=1, source_target_pairs={{1,0},{2,1},{3,2},{4,3},{5,4},{6,5},{7,6},{8,7},{9,8},{10,9},{11,1... | collective-permute-start | bytes 393224 | tf_op jit(solution)/shard_map/ppermute | solution.py:30
  64.4 7.1 %collective-permute-start.3 = (bf16[1,2,32,1024]{3,2,0,1:T(8,128)(2,1)S(1)}, bf16[1,2,32,1024]{3,2,0,1:T(8,128)(2,1)S(1)}, u32[]{:S(2)}, u32[]{:S(2)}) collective-permute-start(bf16[1,2,32,1024]{3,2,0,1:T(8,128)(2,1)S(1)} %get-tuple-element.17), channel_id=1, source_target_pairs={{0,1},{1,2},{2,3},{3,4},{4,5},{5,6},{6,7},{7,8},{8,9},{9,10},{10,1... | collective-permute-start | bytes 393224 | tf_op jit(solution)/shard_map/ppermute | solution.py:29
  64.4 7.1 %collective-permute-start.4 = (bf16[1,2,32,1024]{3,2,0,1:T(8,128)(2,1)S(1)}, bf16[1,2,32,1024]{3,2,0,1:T(8,128)(2,1)S(1)}, u32[]{:S(2)}, u32[]{:S(2)}) collective-permute-start(bf16[1,2,32,1024]{3,2,0,1:T(8,128)(2,1)S(1)} %get-tuple-element.18), channel_id=1, source_target_pairs={{1,0},{2,1},{3,2},{4,3},{5,4},{6,5},{7,6},{8,7},{9,8},{10,9},{11,1... | collective-permute-start | bytes 393224 | tf_op jit(solution)/shard_map/ppermute | solution.py:30
where the time goes:
time: 149 us; the launch traced here: 148 us
  other arithmetic  64.7 us (43%)
  waiting for transfers between devices  36.5 us (24%)
  starting transfers between devices  15.1 us (10%)
  matrix products  13.5 us (9%)
  between operations  13.5 us (9%)
  local copies, waits for them, and re-layouts  4.94 us (3%)
    select_n x1, other arithmetic, regress(): logits = jnp.where(in_band, aggregated, jnp.float32(-1e+30))  35 us
    ppermute x3, waiting for transfers between devices, from_behind(): return lax.ppermute(value, axis, pairs)  34.6 us
    sub x2, other arithmetic, regress(): weights = jnp.where(in_band, jnp.exp(logits - largest), jnp.float32(0.0))  25.6 us
    dot_general x2, matrix products, block_scores(): jnp.einsum('ycnx,ycnj->ynxj', left_blocks, windows, preferred_element_typ...  13.5 us
    ppermute x2, starting transfers between devices, with_halo(): after = lax.ppermute(initial, axis, down)  8.86 us
    ppermute x3, starting transfers between devices, from_behind(): return lax.ppermute(value, axis, pairs)  6.11 us
  transfers between devices with their start and end apart: 7, of which 3 were waited for; matrix products, arithmetic and copies ran while one was open for 3% of the time, Pallas kernels for 0%

commit v1 on v0

v1 whole, which is shorter than its diff:
```python
import math

import jax
import jax.numpy as jnp
from jax import lax
from jax.experimental import pallas as pl
from jax.experimental.pallas import tpu as pltpu
from jax.sharding import PartitionSpec as P

LEVELS = 256
BX = 128
TILES = 4
VIEWS = 4
ROUNDS = 2
PAIRS = ROUNDS * VIEWS
PAD = (TILES - 1) * BX + LEVELS
SCALE = 0.35 * math.log2(math.e)
CHUNKS = (8,)


def slot_of(view, unit):
    return 2 - view if (unit % 2 and view % 2 == 0) else view


def swap_bits(i):
    return ((i & 1) << 1) | (i >> 1)


def tables(strips):
    per_view = strips // VIEWS

    def device(view, unit, core):
        return (view * per_view + 2 * unit + core + per_view // 2) % strips

    units = per_view // 2
    share = []
    for m in range(VIEWS):
        pairs = []
        for unit in range(units):
            order = sorted(range(VIEWS), key=lambda v: slot_of(v, unit))
            for view in range(VIEWS):
                for core in range(2):
                    part = swap_bits(slot_of(view, unit)) ^ m
                    place = 4 * core + part
                    pairs.append((device(view, unit, core), device(order[place // 2], unit, place % 2)))
        share.append(pairs)
    line = []
    for unit in range(units):
        order = sorted(range(VIEWS), key=lambda v: slot_of(v, unit))
        for place in range(8):
            line.append(device(order[place // 2], unit, place % 2))
    down = list(zip(line[:-1], line[1:]))
    return share, down


def regress(scores, half, x_less_b):
    groups = BX // 8

    def part(span, a):
        first = span * BX + 8 * a
        return scores[first : first + 8, half * BX : (half + 1) * BX]

    held = [jnp.where(x_less_b < 8 * a, part(0, a), part(2, a)) for a in range(groups)]
    held += [part(1, a) for a in range(groups)]
    tops = held[:4]
    for i in range(4, 2 * groups):
        tops[i % 4] = jnp.maximum(tops[i % 4], held[i])
    top = jnp.maximum(jnp.maximum(tops[0], tops[1]), jnp.maximum(tops[2], tops[3]))
    top = jnp.broadcast_to(jnp.max(top, axis=0, keepdims=True), (8, BX))
    weights = [jnp.exp2(v - top) for v in held]
    near = weights[groups - 1]
    near_moment = near
    wrapped = jnp.where(x_less_b < 8 * (groups - 1), near, 0.0)
    far = weights[2 * groups - 1]
    far_moment = far
    for a in range(groups - 2, -1, -1):
        near = near + weights[a]
        far = far + weights[groups + a]
        wrapped = jnp.where(x_less_b < 8 * a, near, wrapped)
        if a:
            near_moment = near_moment + near
            far_moment = far_moment + far
    total = near + far
    moment = (
        x_less_b.astype(jnp.float32) * total
        - 8.0 * (near_moment + far_moment)
        + 128.0 * far
        + 256.0 * wrapped
    )
    return jnp.sum(moment, axis=0, keepdims=True) / jnp.sum(total, axis=0, keepdims=True)


def band(numbers, base, above, below, first_block):
    chunks = len(base)
    widths = [a.shape[-1] for a in above]
    channels = above[0].shape[1]
    depth = 4 * channels
    columns = sum(widths)
    count = widths[-1] // BX

    def body(numbers, *refs):
        refs = list(refs)
        base = [[refs.pop(0) for _ in range(VIEWS)] for _ in range(chunks)]
        above = [refs.pop(0) for _ in range(chunks)]
        below = [refs.pop(0) for _ in range(chunks)]
        outs = [refs.pop(0) for _ in range(VIEWS)]
        right, left = refs

        place = numbers[3 * PAIRS]
        unit = place // 8
        bits = place % 4

        def order_of(unit, rank):
            return jnp.where((unit % 2 == 1) & (rank % 2 == 0), 2 - rank, rank)

        def swap(i):
            return (i % 2) * 2 + i // 2

        def view_of(m):
            return order_of(unit, swap(bits ^ m))

        def buffer_of(view, place):
            return (place % 4) ^ swap(order_of(place // 8, view))

        before = jnp.maximum(place - 1, 0)
        after = place + 1
        for m in range(VIEWS):
            view = view_of(m)
            right[m, :PAD, :] = jnp.zeros((PAD, 2 * depth), jnp.bfloat16)
            head, tail = buffer_of(view, before), buffer_of(view, after)
            column = 0
            for c in range(chunks):
                for n in range(widths[c] // BX):
                    span = slice(n * BX, (n + 1) * BX)
                    rows = jnp.concatenate(
                        [above[c][head, :, span], base[c][m][0, :, span], base[c][m][1, :, span], below[c][tail, :, span]],
                        0,
                    )
                    turned = rows.T
                    right[m, PAD + column : PAD + column + BX, :depth] = turned
                    right[m, PAD + column : PAD + column + BX, depth:] = turned
                    column += BX
                    if c < chunks - 1:
                        continue
                    scaled = rows.astype(jnp.float32) * SCALE
                    high = scaled.astype(jnp.bfloat16)
                    low = (scaled - high.astype(jnp.float32)).astype(jnp.bfloat16)
                    for i, value in enumerate((high, low)):
                        quarter = value * jnp.bfloat16(0.25)
                        half = value * jnp.bfloat16(0.5)
                        nothing = jnp.zeros((channels, BX), jnp.bfloat16)
                        q = [quarter[k * channels : (k + 1) * channels] for k in range(4)]
                        h = [half[k * channels : (k + 1) * channels] for k in range(4)]
                        at = slice(i * depth, (i + 1) * depth)
                        left[m, n, at, :BX] = jnp.concatenate([q[0], h[1], q[2], nothing], 0)
                        left[m, n, at, BX:] = jnp.concatenate([nothing, q[1], h[2], q[3]], 0)
        x_less_b = lax.broadcasted_iota(jnp.int32, (8, BX), 1) - lax.broadcasted_iota(jnp.int32, (8, BX), 0)

        for m in range(VIEWS):
            view = view_of(m)

            def one_round(q, carry):
                left_view = numbers[q * VIEWS + view]
                right_view = (left_view + numbers[PAIRS + q * VIEWS + view]) % VIEWS
                tile = numbers[2 * PAIRS + q * VIEWS + view]
                a, b = buffer_of(left_view, place), buffer_of(right_view, place)
                shift = (tile * BX).astype(jnp.float32)
                for n in range(count):
                    start = pl.multiple_of((TILES - 1 + first_block + n - tile) * BX, BX)
                    scores = jnp.dot(
                        right[b, pl.ds(start, BX + LEVELS), :], left[a, n], preferred_element_type=jnp.float32
                    )
                    for r in range(2):
                        outs[m][q, r : r + 1, n * BX : (n + 1) * BX] = regress(scores, r, x_less_b) + shift
                return carry

            lax.fori_loop(0, ROUNDS, one_round, 0)

    vmem = pl.BlockSpec(memory_space=pltpu.VMEM)
    operands = [b for chunk in base for b in chunk] + list(above) + list(below)
    return pl.pallas_call(
        body,
        out_shape=[jax.ShapeDtypeStruct((ROUNDS, 2, widths[-1]), jnp.float32)] * VIEWS,
        in_specs=[pl.BlockSpec(memory_space=pltpu.SMEM)] + [vmem] * len(operands),
        out_specs=[vmem] * VIEWS,
        scratch_shapes=[
            pltpu.VMEM((VIEWS, PAD + columns, 2 * depth), jnp.bfloat16),
            pltpu.VMEM((VIEWS, count, 2 * depth, 2 * BX), jnp.bfloat16),
        ],
        compiler_params=pltpu.CompilerParams(vmem_limit_bytes=48 << 20),
        name="band",
    )(numbers, *operands)


def per_device(features, valid_rows, left_views, right_step, offset_tile):
    row_count, _, col_count = features.shape
    strips = lax.axis_size("strip")
    per_view = strips // VIEWS
    share, down = tables(strips)
    index = (lax.axis_index("strip") - per_view // 2) % strips
    view, spot = index // per_view, index % per_view
    unit, core = spot // 2, spot % 2
    slot = jnp.where((unit % 2 == 1) & (view % 2 == 0), 2 - view, view)
    first = (slot % 2) * 2 + slot // 2
    place = 8 * unit + 2 * slot + core
    numbers = jnp.concatenate(
        [left_views.reshape(-1), right_step.reshape(-1), offset_tile.reshape(-1), place.astype(jnp.int32).reshape(1)]
    )
    row_ids = lax.broadcasted_iota(jnp.int32, (row_count, 1, 1), 0)
    masked = jnp.where(row_ids >= row_count - valid_rows[0], features, jnp.zeros_like(features))
    bounds = [0]
    for blocks in CHUNKS:
        bounds.append(bounds[-1] + blocks * BX)
    base, above, below, results = [], [], [], []
    for c in range(len(CHUNKS)):
        got = []
        for m in range(VIEWS):
            piece = lax.dynamic_slice_in_dim(masked, 2 * (first ^ m), 2, 0)[:, :, bounds[c] : bounds[c + 1]]
            got.append(lax.ppermute(piece, "strip", share[m]))
        base.append(got)
    for c in range(len(CHUNKS)):
        heads = jnp.concatenate([g[:1] for g in base[c]], 0)
        tails = jnp.concatenate([g[1:] for g in base[c]], 0)
        above.append(lax.ppermute(tails, "strip", down))
        below.append(lax.ppermute(heads, "strip", [(j, i) for i, j in down]))
    for c in range(len(CHUNKS)):
        sent = band(numbers, base[: c + 1], above[: c + 1], below[: c + 1], bounds[c] // BX)
        back = [lax.ppermute(sent[m], "strip", [(j, i) for i, j in share[m]]) for m in range(VIEWS)]
        odd = first % 2 == 1
        high = first // 2 == 1
        back = [jnp.where(odd, back[m ^ 1], back[m]) for m in range(VIEWS)]
        back = [jnp.where(high, back[m ^ 2], back[m]) for m in range(VIEWS)]
        results.append(jnp.concatenate(back, 1))
    return jnp.concatenate(results, 2)


def solution(mesh):
    return jax.shard_map(
        per_device,
        mesh=mesh,
        in_specs=(
            P(("groups", "strip"), None, None),
            P(("groups", "strip")),
            P("groups", None),
            P("groups", None),
            P("groups", None),
        ),
        out_specs=P(None, ("groups", "strip"), None),
        check_vma=False,
    )
```

time: 149 us -> 46.2 us (0.31)
  the two profiles are of different devices: /device:TPU:0 before, /device:TPU:7 now
where the time goes in v1:
time: 46.2 us; the launch traced here: 45.9 us
  starting transfers between devices  17.1 us (37%)
  waiting for transfers between devices  15.6 us (34%)
  Pallas kernels  8.15 us (18%)
  local copies, waits for them, and re-layouts  2.2 us (5%)
  other arithmetic  2 us (4%)
  between operations  0.87 us (2%)
    ppermute x4, waiting for transfers between devices, per_device(): got.append(lax.ppermute(piece, 'strip', share[m]))  8.96 us
    pallas_call x1, Pallas kernels, band(): pl.pallas_call(body, out_shape=[jax.ShapeDtypeStruct((ROUNDS, 2, widths[-...  8.15 us
    ppermute x4, starting transfers between devices, per_device(): got.append(lax.ppermute(piece, 'strip', share[m]))  6.82 us
    ppermute x4, starting transfers between devices, per_device(): lax.ppermute(sent[m], 'strip', [(j, i) for i, j in share[m]])  5.89 us
    ppermute x4, waiting for transfers between devices, per_device(): lax.ppermute(sent[m], 'strip', [(j, i) for i, j in share[m]])  3.59 us
    ppermute x1, waiting for transfers between devices, per_device(): below.append(lax.ppermute(heads, 'strip', [(j, i) for i, j in down]))  3.05 us
    ppermute x1, starting transfers between devices, per_device(): below.append(lax.ppermute(heads, 'strip', [(j, i) for i, j in down]))  2.42 us
    ppermute x1, starting transfers between devices, per_device(): above.append(lax.ppermute(tails, 'strip', down))  1.92 us
  transfers between devices with their start and end apart: 10, of which 5 were waited for; matrix products, arithmetic and copies ran while one was open for 1% of the time, Pallas kernels for 0%

profile of v1, /device:TPU:7, one launch (start us, length us, event | category | flops | bytes accessed | tf_op | source)
XLA Modules:
  0.0 45.9 jit_solution(16680113340718631467)
XLA Ops:
  0.7 1.1 %broadcast_select_fusion = bf16[8,32,1024]{2,1,0:T(8,128)(2,1)S(1)} fusion(bf16[8,32,1024]{2,1,0:T(8,128)(2,1)} %param.5, pred[8]{0:T(512)(128)(4,1)S(1)} %iota_compare_fusion), kind=kLoop, calls=%fused_computation | loop fusion | flops 262144 | bytes 1048584 | tf_op jit(solution)/shard_map/jit(_where)/select_n | solution.py:210
  1.9 3.4 %collective-permute-start.3 = (bf16[2,32,1024]{2,1,0:T(8,128)(2,1)S(1)}, bf16[2,32,1024]{2,1,0:T(8,128)(2,1)S(1)}, u32[]{:S(2)}, u32[]{:S(2)}) collective-permute-start(bf16[2,32,1024]{2,1,0:T(8,128)(2,1)S(1)} %get-tuple-element.13), channel_id=1, source_target_pairs={{2,7},{3,15},{6,3},{7,11},{10,6},{11,14},{14,2},{15,10},{4,8},{5,0... | collective-permute-start | bytes 393224 | tf_op jit(solution)/shard_map/ppermute | solution.py:219
  5.3 0.8 %collective-permute-start.2 = (bf16[2,32,1024]{2,1,0:T(8,128)(2,1)S(1)}, bf16[2,32,1024]{2,1,0:T(8,128)(2,1)S(1)}, u32[]{:S(2)}, u32[]{:S(2)}) collective-permute-start(bf16[2,32,1024]{2,1,0:T(8,128)(2,1)S(1)} %get-tuple-element.14), channel_id=1, source_target_pairs={{2,6},{3,14},{6,2},{7,10},{10,7},{11,15},{14,3},{15,11},{4,9},{5,1... | collective-permute-start | bytes 393224 | tf_op jit(solution)/shard_map/ppermute | solution.py:219
  6.1 0.2 collective-permute-start.1
  6.3 2.4 %collective-permute-start = (bf16[2,32,1024]{2,1,0:T(8,128)(2,1)S(1)}, bf16[2,32,1024]{2,1,0:T(8,128)(2,1)S(1)}, u32[]{:S(2)}, u32[]{:S(2)}) collective-permute-start(bf16[2,32,1024]{2,1,0:T(8,128)(2,1)S(1)} %get-tuple-element.16), channel_id=1, source_target_pairs={{2,2},{3,10},{6,6},{7,14},{10,3},{11,11},{14,7},{15,15},{4,13},{5,... | collective-permute-start | bytes 393224 | tf_op jit(solution)/shard_map/ppermute | solution.py:219
  8.8 3.8 %collective-permute-done.2.refs_2_ = bf16[2,32,1024]{2,1,0:T(8,128)(2,1)S(1)} collective-permute-done((bf16[2,32,1024]{2,1,0:T(8,128)(2,1)S(1)}, bf16[2,32,1024]{2,1,0:T(8,128)(2,1)S(1)}, u32[]{:S(2)}, u32[]{:S(2)}) %collective-permute-start.2) | collective-permute-done | bytes 131104 | tf_op jit(solution)/shard_map/ppermute | solution.py:219
  12.6 5.1 %collective-permute-done.refs_0_ = bf16[2,32,1024]{2,1,0:T(8,128)(2,1)S(1)} collective-permute-done((bf16[2,32,1024]{2,1,0:T(8,128)(2,1)S(1)}, bf16[2,32,1024]{2,1,0:T(8,128)(2,1)S(1)}, u32[]{:S(2)}, u32[]{:S(2)}) %collective-permute-start) | collective-permute-done | bytes 131104 | tf_op jit(solution)/shard_map/ppermute | solution.py:219
  17.8 1.9 %collective-permute-start.4 = (bf16[4,32,1024]{2,1,0:T(8,128)(2,1)S(1)}, bf16[4,32,1024]{2,1,0:T(8,128)(2,1)S(1)}, u32[]{:S(2)}, u32[]{:S(2)}) collective-permute-start(bf16[4,32,1024]{2,1,0:T(8,128)(2,1)S(1)} %pad_maximum_fusion), channel_id=1, source_target_pairs={{2,3},{3,6},{6,7},{7,10},{10,11},{11,14},{14,15},{15,12},{12,13},{... | collective-permute-start | bytes 786440 | tf_op jit(solution)/shard_map/ppermute | solution.py:224
  19.8 2.4 %collective-permute-start.5 = (bf16[4,32,1024]{2,1,0:T(8,128)(2,1)S(1)}, bf16[4,32,1024]{2,1,0:T(8,128)(2,1)S(1)}, u32[]{:S(2)}, u32[]{:S(2)}) collective-permute-start(bf16[4,32,1024]{2,1,0:T(8,128)(2,1)S(1)} %pad_maximum_fusion.1), channel_id=1, source_target_pairs={{3,2},{6,3},{7,6},{10,7},{11,10},{14,11},{15,14},{12,15},{13,12},{... | collective-permute-start | bytes 786440 | tf_op jit(solution)/shard_map/ppermute | solution.py:225
  22.2 0.7 %copy-done = s32[2,4]{1,0:T(2,128)S(1)} copy-done((s32[2,4]{1,0:T(2,128)S(1)}, s32[2,4]{1,0:T(2,128)}, u32[]{:S(2)}) %copy-start) | copy-done | bytes 56
  22.9 0.1 reshape.19
  23.0 0.6 %copy-done.1 = s32[2,4]{1,0:T(2,128)S(1)} copy-done((s32[2,4]{1,0:T(2,128)S(1)}, s32[2,4]{1,0:T(2,128)}, u32[]{:S(2)}) %copy-start.1) | copy-done | bytes 56
  23.6 0.1 reshape.20
  23.7 0.6 %copy-done.2 = s32[2,4]{1,0:T(2,128)S(1)} copy-done((s32[2,4]{1,0:T(2,128)S(1)}, s32[2,4]{1,0:T(2,128)}, u32[]{:S(2)}) %copy-start.2) | copy-done | bytes 56
  24.3 0.1 reshape.21
  24.4 0.1 pad_add_fusion.numbers
  24.4 3.1 %collective-permute-done.5.refs_5_ = bf16[4,32,1024]{2,1,0:T(8,128)(2,1)S(1)} collective-permute-done((bf16[4,32,1024]{2,1,0:T(8,128)(2,1)S(1)}, bf16[4,32,1024]{2,1,0:T(8,128)(2,1)S(1)}, u32[]{:S(2)}, u32[]{:S(2)}) %collective-permute-start.5) | collective-permute-done | bytes 262176 | tf_op jit(solution)/shard_map/ppermute | solution.py:225
  27.5 8.2 %band.1 = (f32[2,2,1024]{2,1,0:T(2,128)S(1)}, f32[2,2,1024]{2,1,0:T(2,128)S(1)}, f32[2,2,1024]{2,1,0:T(2,128)S(1)}, f32[2,2,1024]{2,1,0:T(2,128)S(1)}) custom-call(s32[25]{0:T(128)S(1)} %pad_add_fusion.numbers, bf16[2,32,1024]{2,1,0:T(8,128)(2,1)S(1)} %collective-permute-done.refs_0_, bf16[2,32,1024]{2,1,0:T(8,128)(2,1)S(1)} %collective-permute-done.1.refs_1_, ...), custom_call_target="tpu_custom_call" | custom-call | tf_op jit(solution)/shard_map/band/pallas_call | solution.py:181
  35.6 0.1 collective-permute-start.6
  35.7 3.4 %collective-permute-start.7 = (f32[2,2,1024]{2,1,0:T(2,128)S(1)}, f32[2,2,1024]{2,1,0:T(2,128)S(1)}, u32[]{:S(2)}, u32[]{:S(2)}) collective-permute-start(f32[2,2,1024]{2,1,0:T(2,128)S(1)} %get-tuple-element.10), channel_id=1, source_target_pairs={{6,2},{14,3},{2,6},{10,7},{7,10},{15,11},{3,14},{11,15},{9,4},{1,5... | collective-permute-start | bytes 49160 | tf_op jit(solution)/shard_map/ppermute | solution.py:228
  39.1 2.4 %collective-permute-start.9 = (f32[2,2,1024]{2,1,0:T(2,128)S(1)}, f32[2,2,1024]{2,1,0:T(2,128)S(1)}, u32[]{:S(2)}, u32[]{:S(2)}) collective-permute-start(f32[2,2,1024]{2,1,0:T(2,128)S(1)} %get-tuple-element.12), channel_id=1, source_target_pairs={{2,2},{10,3},{6,6},{14,7},{3,10},{11,11},{7,14},{15,15},{13,4},{5,... | collective-permute-start | bytes 49160 | tf_op jit(solution)/shard_map/ppermute | solution.py:228
  41.6 1.0 %collective-permute-done.8 = f32[2,2,1024]{2,1,0:T(2,128)S(1)} collective-permute-done((f32[2,2,1024]{2,1,0:T(2,128)S(1)}, f32[2,2,1024]{2,1,0:T(2,128)S(1)}, u32[]{:S(2)}, u32[]{:S(2)}) %collective-permute-start.8) | collective-permute-done | bytes 16416 | tf_op jit(solution)/shard_map/ppermute | solution.py:228
  42.6 2.6 %collective-permute-done.9 = f32[2,2,1024]{2,1,0:T(2,128)S(1)} collective-permute-done((f32[2,2,1024]{2,1,0:T(2,128)S(1)}, f32[2,2,1024]{2,1,0:T(2,128)S(1)}, u32[]{:S(2)}, u32[]{:S(2)}) %collective-permute-start.9) | collective-permute-done | bytes 16416 | tf_op jit(solution)/shard_map/ppermute | solution.py:228
  45.2 0.7 %pad_maximum_fusion.2 = f32[2,8,1024]{2,1,0:T(8,128)} fusion(f32[2,2,1024]{2,1,0:T(2,128)S(1)} %get-tuple-element.28, f32[2,2,1024]{2,1,0:T(2,128)S(1)} %get-tuple-element.27, f32[2,2,1024]{2,1,0:T(2,128)S(1)} %get-tuple-element.26, f32[2,2,1024]{2,1,0:T(2,128)S(1)} %get-tuple-element.25), kind=kLoop, calls=%fused_computation.3 | loop fusion | flops 49152 | bytes 131072 | tf_op jit(solution)/shard_map/concatenate | solution.py:233
  (18 shorter events, 0.2 us)
Async XLA Ops:
  1.9 6.8 %collective-permute-start.3 = (bf16[2,32,1024]{2,1,0:T(8,128)(2,1)S(1)}, bf16[2,32,1024]{2,1,0:T(8,128)(2,1)S(1)}, u32[]{:S(2)}, u32[]{:S(2)}) collective-permute-start(bf16[2,32,1024]{2,1,0:T(8,128)(2,1)S(1)} %get-tuple-element.13), channel_id=1, source_target_pairs={{2,7},{3,15},{6,3},{7,11},{10,6},{11,14},{14,2},{15,10},{4,8},{5,0... | collective-permute-start | bytes 393224 | tf_op jit(solution)/shard_map/ppermute | solution.py:219
  5.3 7.3 %collective-permute-start.2 = (bf16[2,32,1024]{2,1,0:T(8,128)(2,1)S(1)}, bf16[2,32,1024]{2,1,0:T(8,128)(2,1)S(1)}, u32[]{:S(2)}, u32[]{:S(2)}) collective-permute-start(bf16[2,32,1024]{2,1,0:T(8,128)(2,1)S(1)} %get-tuple-element.14), channel_id=1, source_target_pairs={{2,6},{3,14},{6,2},{7,10},{10,7},{11,15},{14,3},{15,11},{4,9},{5,1... | collective-permute-start | bytes 393224 | tf_op jit(solution)/shard_map/ppermute | solution.py:219
  6.1 6.5 %collective-permute-start.1 = (bf16[2,32,1024]{2,1,0:T(8,128)(2,1)S(1)}, bf16[2,32,1024]{2,1,0:T(8,128)(2,1)S(1)}, u32[]{:S(2)}, u32[]{:S(2)}) collective-permute-start(bf16[2,32,1024]{2,1,0:T(8,128)(2,1)S(1)} %get-tuple-element.15), channel_id=1, source_target_pairs={{2,3},{3,11},{6,7},{7,15},{10,2},{11,10},{14,6},{15,14},{4,12},{5,... | collective-permute-start | bytes 393224 | tf_op jit(solution)/shard_map/ppermute | solution.py:219
  6.3 11.5 %collective-permute-start = (bf16[2,32,1024]{2,1,0:T(8,128)(2,1)S(1)}, bf16[2,32,1024]{2,1,0:T(8,128)(2,1)S(1)}, u32[]{:S(2)}, u32[]{:S(2)}) collective-permute-start(bf16[2,32,1024]{2,1,0:T(8,128)(2,1)S(1)} %get-tuple-element.16), channel_id=1, source_target_pairs={{2,2},{3,10},{6,6},{7,14},{10,3},{11,11},{14,7},{15,15},{4,13},{5,... | collective-permute-start | bytes 393224 | tf_op jit(solution)/shard_map/ppermute | solution.py:219
  17.8 6.6 %collective-permute-start.4 = (bf16[4,32,1024]{2,1,0:T(8,128)(2,1)S(1)}, bf16[4,32,1024]{2,1,0:T(8,128)(2,1)S(1)}, u32[]{:S(2)}, u32[]{:S(2)}) collective-permute-start(bf16[4,32,1024]{2,1,0:T(8,128)(2,1)S(1)} %pad_maximum_fusion), channel_id=1, source_target_pairs={{2,3},{3,6},{6,7},{7,10},{10,11},{11,14},{14,15},{15,12},{12,13},{... | collective-permute-start | bytes 786440 | tf_op jit(solution)/shard_map/ppermute | solution.py:224
  19.8 7.7 %collective-permute-start.5 = (bf16[4,32,1024]{2,1,0:T(8,128)(2,1)S(1)}, bf16[4,32,1024]{2,1,0:T(8,128)(2,1)S(1)}, u32[]{:S(2)}, u32[]{:S(2)}) collective-permute-start(bf16[4,32,1024]{2,1,0:T(8,128)(2,1)S(1)} %pad_maximum_fusion.1), channel_id=1, source_target_pairs={{3,2},{6,3},{7,6},{10,7},{11,10},{14,11},{15,14},{12,15},{13,12},{... | collective-permute-start | bytes 786440 | tf_op jit(solution)/shard_map/ppermute | solution.py:225
  22.2 0.7 %copy-start = (s32[2,4]{1,0:T(2,128)S(1)}, s32[2,4]{1,0:T(2,128)}, u32[]{:S(2)}) copy-start(s32[2,4]{1,0:T(2,128)} %param.7) | copy-start | bytes 100
  22.9 0.7 %copy-start.1 = (s32[2,4]{1,0:T(2,128)S(1)}, s32[2,4]{1,0:T(2,128)}, u32[]{:S(2)}) copy-start(s32[2,4]{1,0:T(2,128)} %param.8) | copy-start | bytes 100
  23.6 0.7 %copy-start.2 = (s32[2,4]{1,0:T(2,128)S(1)}, s32[2,4]{1,0:T(2,128)}, u32[]{:S(2)}) copy-start(s32[2,4]{1,0:T(2,128)} %param.9) | copy-start | bytes 100
  35.6 5.9 %collective-permute-start.6 = (f32[2,2,1024]{2,1,0:T(2,128)S(1)}, f32[2,2,1024]{2,1,0:T(2,128)S(1)}, u32[]{:S(2)}, u32[]{:S(2)}) collective-permute-start(f32[2,2,1024]{2,1,0:T(2,128)S(1)} %get-tuple-element.9), channel_id=1, source_target_pairs={{7,2},{15,3},{3,6},{11,7},{6,10},{14,11},{2,14},{10,15},{8,4},{0,5... | collective-permute-start | bytes 49160 | tf_op jit(solution)/shard_map/ppermute | solution.py:228
  35.7 5.9 %collective-permute-start.7 = (f32[2,2,1024]{2,1,0:T(2,128)S(1)}, f32[2,2,1024]{2,1,0:T(2,128)S(1)}, u32[]{:S(2)}, u32[]{:S(2)}) collective-permute-start(f32[2,2,1024]{2,1,0:T(2,128)S(1)} %get-tuple-element.10), channel_id=1, source_target_pairs={{6,2},{14,3},{2,6},{10,7},{7,10},{15,11},{3,14},{11,15},{9,4},{1,5... | collective-permute-start | bytes 49160 | tf_op jit(solution)/shard_map/ppermute | solution.py:228
  39.1 3.5 %collective-permute-start.8 = (f32[2,2,1024]{2,1,0:T(2,128)S(1)}, f32[2,2,1024]{2,1,0:T(2,128)S(1)}, u32[]{:S(2)}, u32[]{:S(2)}) collective-permute-start(f32[2,2,1024]{2,1,0:T(2,128)S(1)} %get-tuple-element.11), channel_id=1, source_target_pairs={{3,2},{11,3},{7,6},{15,7},{2,10},{10,11},{6,14},{14,15},{12,4},{4,... | collective-permute-start | bytes 49160 | tf_op jit(solution)/shard_map/ppermute | solution.py:228
  39.1 6.1 %collective-permute-start.9 = (f32[2,2,1024]{2,1,0:T(2,128)S(1)}, f32[2,2,1024]{2,1,0:T(2,128)S(1)}, u32[]{:S(2)}, u32[]{:S(2)}) collective-permute-start(f32[2,2,1024]{2,1,0:T(2,128)S(1)} %get-tuple-element.12), channel_id=1, source_target_pairs={{2,2},{10,3},{6,6},{14,7},{3,10},{11,11},{7,14},{15,15},{13,4},{5,... | collective-permute-start | bytes 49160 | tf_op jit(solution)/shard_map/ppermute | solution.py:228

commit v2 on v1

v2 whole, which is shorter than its diff:
```python
import math

import jax
import jax.numpy as jnp
from jax import lax
from jax.experimental import pallas as pl
from jax.experimental.pallas import tpu as pltpu
from jax.sharding import PartitionSpec as P

LEVELS = 256
BX = 128
TILES = 4
VIEWS = 4
ROUNDS = 2
PAIRS = ROUNDS * VIEWS
FLIP = 3
PAD = (TILES - 1) * BX + LEVELS
SCALE = 0.35 * math.log2(math.e)


def slot_of(view, unit):
    return 2 - view if (unit % 2 and view % 2 == 0) else view


def swap_bits(i):
    return ((i & 1) << 1) | (i >> 1)


def tables(strips):
    per_view = strips // VIEWS

    def device(view, unit, core):
        return (view * per_view + 2 * unit + core + per_view // 2) % strips

    units = per_view // 2
    share = []
    for m in range(VIEWS):
        pairs = []
        for unit in range(units):
            order = sorted(range(VIEWS), key=lambda v: slot_of(v, unit))
            for view in range(VIEWS):
                for core in range(2):
                    part = swap_bits(slot_of(view, unit)) ^ m ^ FLIP
                    place = 4 * core + part
                    pairs.append((device(view, unit, core), device(order[place // 2], unit, place % 2)))
        share.append(pairs)
    line = []
    for unit in range(units):
        order = sorted(range(VIEWS), key=lambda v: slot_of(v, unit))
        for place in range(8):
            line.append(device(order[place // 2], unit, place % 2))
    inner = [(line[i], line[i ^ 1]) for i in range(len(line))]
    outer = [(line[i], line[i + 1]) for i in range(1, len(line) - 1, 2)]
    return share, inner, outer + [(j, i) for i, j in outer]


def regress(scores, half, x_less_b):
    groups = BX // 8

    def part(span, a):
        first = (span + half) * BX + 8 * a
        return scores[first : first + 8, half * BX : (half + 1) * BX]

    held = [jnp.where(x_less_b < 8 * a, part(0, a), part(2, a)) for a in range(groups)]
    held += [part(1, a) for a in range(groups)]
    tops = held[:4]
    for i in range(4, 2 * groups):
        tops[i % 4] = jnp.maximum(tops[i % 4], held[i])
    top = jnp.maximum(jnp.maximum(tops[0], tops[1]), jnp.maximum(tops[2], tops[3]))
    top = jnp.broadcast_to(jnp.max(top, axis=0, keepdims=True), (8, BX))
    weights = [jnp.exp2((v - top) * SCALE) for v in held]
    near = weights[groups - 1]
    near_moment = near
    wrapped = jnp.where(x_less_b < 8 * (groups - 1), near, 0.0)
    far = weights[2 * groups - 1]
    far_moment = far
    for a in range(groups - 2, -1, -1):
        near = near + weights[a]
        far = far + weights[groups + a]
        wrapped = jnp.where(x_less_b < 8 * a, near, wrapped)
        if a:
            near_moment = near_moment + near
            far_moment = far_moment + far
    total = near + far
    moment = (
        x_less_b.astype(jnp.float32) * total
        - 8.0 * (near_moment + far_moment)
        + 128.0 * far
        + 256.0 * wrapped
    )
    return jnp.sum(moment, axis=0, keepdims=True) / jnp.sum(total, axis=0, keepdims=True)


def band(numbers, base, rim, done):
    inner = done is None
    _, channels, columns = base[0].shape
    depth = 4 * channels

    def body(numbers, *refs):
        base, rim = refs[:VIEWS], refs[VIEWS]
        if inner:
            result, right, left = refs[VIEWS + 1 :]
        else:
            done = refs[VIEWS + 1]
            outs = refs[VIEWS + 2 : 2 * VIEWS + 2]
            right, left, result = refs[2 * VIEWS + 2 :]

        place = numbers[3 * PAIRS]
        core = place % 2

        def order_of(unit, rank):
            return jnp.where((unit % 2 == 1) & (rank % 2 == 0), 2 - rank, rank)

        def swap(i):
            return (i % 2) * 2 + i // 2

        def view_of(m):
            return order_of(place // 8, swap((place % 4) ^ m ^ FLIP))

        def buffer_of(view, place):
            return (place % 4) ^ swap(order_of(place // 8, view)) ^ FLIP

        sender = place + 1 - 2 * core if inner else jnp.maximum(place - 1 + 2 * core, 0)
        middle = 1 - core if inner else core
        heavy = 0.25 + 0.25 * middle.astype(jnp.float32)
        shares = [jnp.full((channels, BX), w).astype(jnp.bfloat16) for w in (0.75 - heavy, heavy, 0.25)]
        nothing = jnp.zeros((channels, BX), jnp.bfloat16)
        for m in range(VIEWS):
            there = buffer_of(view_of(m), sender)
            right[m, :PAD, :] = jnp.zeros((PAD, depth), jnp.bfloat16)
            for n in range(columns // BX):
                span = slice(n * BX, (n + 1) * BX)
                rows = [base[m][0, :, span], base[m][1, :, span], rim[there, :, span]]
                right[m, PAD + n * BX : PAD + (n + 1) * BX, :] = jnp.concatenate(rows + [nothing], 0).T
                left[m, :, span] = jnp.concatenate([r * w for r, w in zip(rows, shares)] + [nothing], 0)
        x_less_b = lax.broadcasted_iota(jnp.int32, (8, BX), 1) - lax.broadcasted_iota(jnp.int32, (8, BX), 0)

        def one_pair(j, carry):
            view = j % VIEWS
            left_view = numbers[j]
            right_view = (left_view + numbers[PAIRS + j]) % VIEWS
            tile = numbers[2 * PAIRS + j]
            a, b = buffer_of(left_view, place), buffer_of(right_view, place)
            shift = (tile * BX).astype(jnp.float32)
            home = ROUNDS * buffer_of(view, place) + j // VIEWS
            for n in range(0, columns // BX, 2):
                start = pl.multiple_of((TILES - 1 + n - tile) * BX, BX)
                scores = jnp.dot(
                    right[b, pl.ds(start, 2 * BX + LEVELS), :],
                    left[a, :, n * BX : (n + 2) * BX],
                    preferred_element_type=jnp.float32,
                )
                for i in range(2):
                    result[home, :, (n + i) * BX : (n + i + 1) * BX] = regress(scores, i, x_less_b) + shift
            return carry

        lax.fori_loop(0, PAIRS, one_pair, 0, unroll=4)
        if not inner:
            for m in range(VIEWS):
                for q in range(ROUNDS):
                    both = [done[ROUNDS * m + q], result[ROUNDS * m + q]]
                    outs[m][q, 0:1, :] = jnp.where(core == 0, both[1], both[0])
                    outs[m][q, 1:2, :] = jnp.where(core == 0, both[0], both[1])

    vmem = pl.BlockSpec(memory_space=pltpu.VMEM)
    operands = list(base) + [rim] + ([] if inner else [done])
    every = jax.ShapeDtypeStruct((PAIRS, 1, columns), jnp.float32)
    scratch = [pltpu.VMEM((VIEWS, PAD + columns, depth), jnp.bfloat16), pltpu.VMEM((VIEWS, depth, columns), jnp.bfloat16)]
    return pl.pallas_call(
        body,
        out_shape=every if inner else [jax.ShapeDtypeStruct((ROUNDS, 2, columns), jnp.float32)] * VIEWS,
        in_specs=[pl.BlockSpec(memory_space=pltpu.SMEM)] + [vmem] * len(operands),
        out_specs=vmem if inner else [vmem] * VIEWS,
        scratch_shapes=scratch if inner else scratch + [pltpu.VMEM(every.shape, every.dtype)],
        compiler_params=pltpu.CompilerParams(vmem_limit_bytes=48 << 20),
        name="band_inner" if inner else "band_outer",
    )(numbers, *operands)


def per_device(features, valid_rows, left_views, right_step, offset_tile):
    row_count = features.shape[0]
    strips = lax.axis_size("strip")
    per_view = strips // VIEWS
    share, siblings, neighbours = tables(strips)
    index = (lax.axis_index("strip") - per_view // 2) % strips
    view, spot = index // per_view, index % per_view
    unit, core = spot // 2, spot % 2
    slot = jnp.where((unit % 2 == 1) & (view % 2 == 0), 2 - view, view)
    first = ((slot % 2) * 2 + slot // 2) ^ FLIP
    place = 8 * unit + 2 * slot + core
    numbers = jnp.concatenate(
        [left_views.reshape(-1), right_step.reshape(-1), offset_tile.reshape(-1), place.astype(jnp.int32).reshape(1)]
    )
    row_ids = lax.broadcasted_iota(jnp.int32, (row_count, 1, 1), 0)
    masked = jnp.where(row_ids >= row_count - valid_rows[0], features, jnp.zeros_like(features))
    base = []
    for m in range(VIEWS):
        base.append(lax.ppermute(lax.dynamic_slice_in_dim(masked, 2 * (first ^ m), 2, 0), "strip", share[m]))
    numbers, base = lax.optimization_barrier((numbers, base))
    rows = [jnp.concatenate([lax.dynamic_slice_in_dim(g, r, 1, 0) for g in base], 0) for r in (1 - core, core)]
    beside = lax.ppermute(rows[0], "strip", siblings)
    beyond = lax.ppermute(rows[1], "strip", neighbours)
    sent = band(numbers, base, beyond, band(numbers, base, beside, None))
    back = [lax.ppermute(sent[m], "strip", [(j, i) for i, j in share[m]]) for m in range(VIEWS)]
    back = [jnp.where(first % 2 == 1, back[m ^ 1], back[m]) for m in range(VIEWS)]
    back = [jnp.where(first // 2 == 1, back[m ^ 2], back[m]) for m in range(VIEWS)]
    return jnp.concatenate(back, 1)


def solution(mesh):
    return jax.shard_map(
        per_device,
        mesh=mesh,
        in_specs=(
            P(("groups", "strip"), None, None),
            P(("groups", "strip")),
            P("groups", None),
            P("groups", None),
            P("groups", None),
        ),
        out_specs=P(None, ("groups", "strip"), None),
        check_vma=False,
    )
```

time: 46.2 us -> 41.8 us (0.905)
  the two profiles are of different devices: /device:TPU:7 before, /device:TPU:0 now
where the time goes in v2:
time: 41.8 us; the launch traced here: 41.5 us
  starting transfers between devices  16.7 us (40%)
  waiting for transfers between devices  11.7 us (28%)
  Pallas kernels  8.08 us (19%)
  local copies, waits for them, and re-layouts  2.21 us (5%)
  other arithmetic  2 us (5%)
  between operations  0.82 us (2%)
    pallas_call x2, Pallas kernels, band(): pl.pallas_call(body, out_shape=every if inner else [jax.ShapeDtypeStruct(...  8.08 us
    ppermute x4, starting transfers between devices, per_device(): lax.ppermute(lax.dynamic_slice_in_dim(masked, 2 * (first ^ m), 2, 0), 'st...  7.74 us
    ppermute x4, waiting for transfers between devices, per_device(): lax.ppermute(lax.dynamic_slice_in_dim(masked, 2 * (first ^ m), 2, 0), 'st...  6.2 us
    ppermute x4, starting transfers between devices, per_device(): lax.ppermute(sent[m], 'strip', [(j, i) for i, j in share[m]])  6.07 us
    ppermute x4, waiting for transfers between devices, per_device(): lax.ppermute(sent[m], 'strip', [(j, i) for i, j in share[m]])  4.64 us
    ppermute x1, starting transfers between devices, per_device(): beyond = lax.ppermute(rows[1], 'strip', neighbours)  2.8 us
    unnamed x6, local copies, waits for them, and re-layouts  1.87 us
    select_n x1, other arithmetic, per_device(): jnp.where(row_ids >= row_count - valid_rows[0], features, jnp.zeros_like(...  1.15 us
  transfers between devices with their start and end apart: 10, of which 6 were waited for; matrix products, arithmetic and copies ran while one was open for 1% of the time, Pallas kernels for 10%

profile of v2, /device:TPU:0, one launch (start us, length us, event | category | flops | bytes accessed | tf_op | source)
XLA Modules:
  0.0 41.5 jit_solution(8186985441643478787)
XLA Ops:
  0.7 1.1 %broadcast_select_fusion = bf16[8,32,1024]{2,1,0:T(8,128)(2,1)S(1)} fusion(bf16[8,32,1024]{2,1,0:T(8,128)(2,1)} %param.5, pred[8]{0:T(512)(128)(4,1)S(1)} %iota_compare_fusion), kind=kLoop, calls=%fused_computation | loop fusion | flops 262144 | bytes 1048584 | tf_op jit(solution)/shard_map/jit(_where)/select_n | solution.py:195
  1.9 5.1 %collective-permute-start = (bf16[2,32,1024]{2,1,0:T(8,128)(2,1)S(1)}, bf16[2,32,1024]{2,1,0:T(8,128)(2,1)S(1)}, u32[]{:S(2)}, u32[]{:S(2)}) collective-permute-start(bf16[2,32,1024]{2,1,0:T(8,128)(2,1)S(1)} %get-tuple-element.26), channel_id=1, source_target_pairs={{2,7},{3,15},{6,3},{7,11},{10,6},{11,14},{14,2},{15,10},{4,8},{5,0... | collective-permute-start | bytes 393224 | tf_op jit(solution)/shard_map/ppermute | solution.py:198
  7.0 0.6 %collective-permute-start.2 = (bf16[2,32,1024]{2,1,0:T(8,128)(2,1)S(1)}, bf16[2,32,1024]{2,1,0:T(8,128)(2,1)S(1)}, u32[]{:S(2)}, u32[]{:S(2)}) collective-permute-start(bf16[2,32,1024]{2,1,0:T(8,128)(2,1)S(1)} %get-tuple-element.24), channel_id=1, source_target_pairs={{2,3},{3,11},{6,7},{7,15},{10,2},{11,10},{14,6},{15,14},{4,12},{5,... | collective-permute-start | bytes 393224 | tf_op jit(solution)/shard_map/ppermute | solution.py:198
  7.7 2.0 %collective-permute-start.3 = (bf16[2,32,1024]{2,1,0:T(8,128)(2,1)S(1)}, bf16[2,32,1024]{2,1,0:T(8,128)(2,1)S(1)}, u32[]{:S(2)}, u32[]{:S(2)}) collective-permute-start(bf16[2,32,1024]{2,1,0:T(8,128)(2,1)S(1)} %get-tuple-element.23), channel_id=1, source_target_pairs={{2,2},{3,10},{6,6},{7,14},{10,3},{11,11},{14,7},{15,15},{4,13},{5,... | collective-permute-start | bytes 393224 | tf_op jit(solution)/shard_map/ppermute | solution.py:198
  9.7 0.7 %copy-done = s32[2,4]{1,0:T(2,128)S(1)} copy-done((s32[2,4]{1,0:T(2,128)S(1)}, s32[2,4]{1,0:T(2,128)}, u32[]{:S(2)}) %copy-start) | copy-done | bytes 56
  10.4 0.1 reshape.19
  10.4 0.6 %copy-done.1 = s32[2,4]{1,0:T(2,128)S(1)} copy-done((s32[2,4]{1,0:T(2,128)S(1)}, s32[2,4]{1,0:T(2,128)}, u32[]{:S(2)}) %copy-start.1) | copy-done | bytes 56
  11.0 0.1 reshape.20
  11.1 0.6 %copy-done.2 = s32[2,4]{1,0:T(2,128)S(1)} copy-done((s32[2,4]{1,0:T(2,128)S(1)}, s32[2,4]{1,0:T(2,128)}, u32[]{:S(2)}) %copy-start.2) | copy-done | bytes 56
  11.7 0.1 reshape.21
  11.8 0.1 pad_add_fusion.numbers
  11.9 1.5 %collective-permute-done.1.refs_1_ = bf16[2,32,1024]{2,1,0:T(8,128)(2,1)S(1)} collective-permute-done((bf16[2,32,1024]{2,1,0:T(8,128)(2,1)S(1)}, bf16[2,32,1024]{2,1,0:T(8,128)(2,1)S(1)}, u32[]{:S(2)}, u32[]{:S(2)}) %collective-permute-start.1) | collective-permute-done | bytes 131104 | tf_op jit(solution)/shard_map/ppermute | solution.py:198
  13.4 4.7 %collective-permute-done.3.refs_3_ = bf16[2,32,1024]{2,1,0:T(8,128)(2,1)S(1)} collective-permute-done((bf16[2,32,1024]{2,1,0:T(8,128)(2,1)S(1)}, bf16[2,32,1024]{2,1,0:T(8,128)(2,1)S(1)}, u32[]{:S(2)}, u32[]{:S(2)}) %collective-permute-start.3) | collective-permute-done | bytes 131104 | tf_op jit(solution)/shard_map/ppermute | solution.py:198
  18.3 2.8 %collective-permute-start.4 = (bf16[4,32,1024]{2,1,0:T(8,128)(2,1)S(1)}, bf16[4,32,1024]{2,1,0:T(8,128)(2,1)S(1)}, u32[]{:S(2)}, u32[]{:S(2)}) collective-permute-start(bf16[4,32,1024]{2,1,0:T(8,128)(2,1)S(1)} %pad_maximum_fusion), channel_id=1, source_target_pairs={{3,6},{7,10},{11,14},{15,12},{13,8},{9,4},{5,0},{6,3},{10,7},{14,1... | collective-permute-start | bytes 786440 | tf_op jit(solution)/shard_map/ppermute | solution.py:202
  21.1 4.0 %band_inner.1.refs_5_ = f32[8,1,1024]{2,1,0:T(1,128)S(1)} custom-call(s32[25]{0:T(128)S(1)} %pad_add_fusion.numbers, bf16[2,32,1024]{2,1,0:T(8,128)(2,1)S(1)} %collective-permute-done.refs_0_, bf16[2,32,1024]{2,1,0:T(8,128)(2,1)S(1)} %collective-permute-done.1.refs_1_, bf16[2,32,1024]{2,1,0:T(8,128)(2,1)S(1)} %collective-permute-done.2.refs_2_, ...), custom_call_target="tpu_custom_call" | custom-call | tf_op jit(solution)/shard_map/band_inner/pallas_call | solution.py:169
  25.2 0.9 %collective-permute-done.4.refs_4_ = bf16[4,32,1024]{2,1,0:T(8,128)(2,1)S(1)} collective-permute-done((bf16[4,32,1024]{2,1,0:T(8,128)(2,1)S(1)}, bf16[4,32,1024]{2,1,0:T(8,128)(2,1)S(1)}, u32[]{:S(2)}, u32[]{:S(2)}) %collective-permute-start.4) | collective-permute-done | bytes 262176 | tf_op jit(solution)/shard_map/ppermute | solution.py:202
  26.0 4.1 %band_outer.1 = (f32[2,2,1024]{2,1,0:T(2,128)S(1)}, f32[2,2,1024]{2,1,0:T(2,128)S(1)}, f32[2,2,1024]{2,1,0:T(2,128)S(1)}, f32[2,2,1024]{2,1,0:T(2,128)S(1)}) custom-call(s32[25]{0:T(128)S(1)} %pad_add_fusion.numbers, bf16[2,32,1024]{2,1,0:T(8,128)(2,1)S(1)} %collective-permute-done.refs_0_, bf16[2,32,1024]{2,1,0:T(8,128)(2,1)S(1)} %collective-permute-done.1.refs_1_, ...), custom_call_target="tpu_custom_call" | custom-call | tf_op jit(solution)/shard_map/band_outer/pallas_call | solution.py:169
  30.1 2.4 %collective-permute-start.6 = (f32[2,2,1024]{2,1,0:T(2,128)S(1)}, f32[2,2,1024]{2,1,0:T(2,128)S(1)}, u32[]{:S(2)}, u32[]{:S(2)}) collective-permute-start(f32[2,2,1024]{2,1,0:T(2,128)S(1)} %get-tuple-element.19), channel_id=1, source_target_pairs={{2,2},{10,3},{6,6},{14,7},{3,10},{11,11},{7,14},{15,15},{13,4},{5,... | collective-permute-start | bytes 49160 | tf_op jit(solution)/shard_map/ppermute | solution.py:204
  32.6 2.7 %collective-permute-start.8 = (f32[2,2,1024]{2,1,0:T(2,128)S(1)}, f32[2,2,1024]{2,1,0:T(2,128)S(1)}, u32[]{:S(2)}, u32[]{:S(2)}) collective-permute-start(f32[2,2,1024]{2,1,0:T(2,128)S(1)} %get-tuple-element.21), channel_id=1, source_target_pairs={{6,2},{14,3},{2,6},{10,7},{7,10},{15,11},{3,14},{11,15},{9,4},{1,5... | collective-permute-start | bytes 49160 | tf_op jit(solution)/shard_map/ppermute | solution.py:204
  35.3 0.9 %collective-permute-start.9 = (f32[2,2,1024]{2,1,0:T(2,128)S(1)}, f32[2,2,1024]{2,1,0:T(2,128)S(1)}, u32[]{:S(2)}, u32[]{:S(2)}) collective-permute-start(f32[2,2,1024]{2,1,0:T(2,128)S(1)} %get-tuple-element.22), channel_id=1, source_target_pairs={{7,2},{15,3},{3,6},{11,7},{6,10},{14,11},{2,14},{10,15},{8,4},{0,5... | collective-permute-start | bytes 49160 | tf_op jit(solution)/shard_map/ppermute | solution.py:204
  36.2 1.1 %collective-permute-done.7 = f32[2,2,1024]{2,1,0:T(2,128)S(1)} collective-permute-done((f32[2,2,1024]{2,1,0:T(2,128)S(1)}, f32[2,2,1024]{2,1,0:T(2,128)S(1)}, u32[]{:S(2)}, u32[]{:S(2)}) %collective-permute-start.7) | collective-permute-done | bytes 16416 | tf_op jit(solution)/shard_map/ppermute | solution.py:204
  37.2 0.5 %collective-permute-done.8 = f32[2,2,1024]{2,1,0:T(2,128)S(1)} collective-permute-done((f32[2,2,1024]{2,1,0:T(2,128)S(1)}, f32[2,2,1024]{2,1,0:T(2,128)S(1)}, u32[]{:S(2)}, u32[]{:S(2)}) %collective-permute-start.8) | collective-permute-done | bytes 16416 | tf_op jit(solution)/shard_map/ppermute | solution.py:204
  37.7 3.1 %collective-permute-done.9 = f32[2,2,1024]{2,1,0:T(2,128)S(1)} collective-permute-done((f32[2,2,1024]{2,1,0:T(2,128)S(1)}, f32[2,2,1024]{2,1,0:T(2,128)S(1)}, u32[]{:S(2)}, u32[]{:S(2)}) %collective-permute-start.9) | collective-permute-done | bytes 16416 | tf_op jit(solution)/shard_map/ppermute | solution.py:204
  40.8 0.7 %pad_maximum_fusion.2 = f32[2,8,1024]{2,1,0:T(8,128)} fusion(f32[2,2,1024]{2,1,0:T(2,128)S(1)} %get-tuple-element.38, f32[2,2,1024]{2,1,0:T(2,128)S(1)} %get-tuple-element.37, f32[2,2,1024]{2,1,0:T(2,128)S(1)} %get-tuple-element.36, f32[2,2,1024]{2,1,0:T(2,128)S(1)} %get-tuple-element.35), kind=kLoop, calls=%fused_computation.3 | loop fusion | flops 49152 | bytes 131072 | tf_op jit(solution)/shard_map/concatenate | solution.py:207
  (17 shorter events, 0.4 us)
Async XLA Ops:
  1.9 10.0 %collective-permute-start = (bf16[2,32,1024]{2,1,0:T(8,128)(2,1)S(1)}, bf16[2,32,1024]{2,1,0:T(8,128)(2,1)S(1)}, u32[]{:S(2)}, u32[]{:S(2)}) collective-permute-start(bf16[2,32,1024]{2,1,0:T(8,128)(2,1)S(1)} %get-tuple-element.26), channel_id=1, source_target_pairs={{2,7},{3,15},{6,3},{7,11},{10,6},{11,14},{14,2},{15,10},{4,8},{5,0... | collective-permute-start | bytes 393224 | tf_op jit(solution)/shard_map/ppermute | solution.py:198
  7.0 6.4 %collective-permute-start.1 = (bf16[2,32,1024]{2,1,0:T(8,128)(2,1)S(1)}, bf16[2,32,1024]{2,1,0:T(8,128)(2,1)S(1)}, u32[]{:S(2)}, u32[]{:S(2)}) collective-permute-start(bf16[2,32,1024]{2,1,0:T(8,128)(2,1)S(1)} %get-tuple-element.25), channel_id=1, source_target_pairs={{2,6},{3,14},{6,2},{7,10},{10,7},{11,15},{14,3},{15,11},{4,9},{5,1... | collective-permute-start | bytes 393224 | tf_op jit(solution)/shard_map/ppermute | solution.py:198
  7.0 6.4 %collective-permute-start.2 = (bf16[2,32,1024]{2,1,0:T(8,128)(2,1)S(1)}, bf16[2,32,1024]{2,1,0:T(8,128)(2,1)S(1)}, u32[]{:S(2)}, u32[]{:S(2)}) collective-permute-start(bf16[2,32,1024]{2,1,0:T(8,128)(2,1)S(1)} %get-tuple-element.24), channel_id=1, source_target_pairs={{2,3},{3,11},{6,7},{7,15},{10,2},{11,10},{14,6},{15,14},{4,12},{5,... | collective-permute-start | bytes 393224 | tf_op jit(solution)/shard_map/ppermute | solution.py:198
  7.7 10.4 %collective-permute-start.3 = (bf16[2,32,1024]{2,1,0:T(8,128)(2,1)S(1)}, bf16[2,32,1024]{2,1,0:T(8,128)(2,1)S(1)}, u32[]{:S(2)}, u32[]{:S(2)}) collective-permute-start(bf16[2,32,1024]{2,1,0:T(8,128)(2,1)S(1)} %get-tuple-element.23), channel_id=1, source_target_pairs={{2,2},{3,10},{6,6},{7,14},{10,3},{11,11},{14,7},{15,15},{4,13},{5,... | collective-permute-start | bytes 393224 | tf_op jit(solution)/shard_map/ppermute | solution.py:198
  9.7 0.7 %copy-start = (s32[2,4]{1,0:T(2,128)S(1)}, s32[2,4]{1,0:T(2,128)}, u32[]{:S(2)}) copy-start(s32[2,4]{1,0:T(2,128)} %param.7) | copy-start | bytes 100
  10.4 0.7 %copy-start.1 = (s32[2,4]{1,0:T(2,128)S(1)}, s32[2,4]{1,0:T(2,128)}, u32[]{:S(2)}) copy-start(s32[2,4]{1,0:T(2,128)} %param.8) | copy-start | bytes 100
  11.0 0.7 %copy-start.2 = (s32[2,4]{1,0:T(2,128)S(1)}, s32[2,4]{1,0:T(2,128)}, u32[]{:S(2)}) copy-start(s32[2,4]{1,0:T(2,128)} %param.9) | copy-start | bytes 100
  18.2 2.9 %collective-permute-start.5 = (bf16[4,32,1024]{2,1,0:T(8,128)(2,1)S(1)}, bf16[4,32,1024]{2,1,0:T(8,128)(2,1)S(1)}, u32[]{:S(2)}, u32[]{:S(2)}) collective-permute-start(bf16[4,32,1024]{2,1,0:T(8,128)(2,1)S(1)} %pad_maximum_fusion.1), channel_id=1, source_target_pairs={{2,3},{3,2},{6,7},{7,6},{10,11},{11,10},{14,15},{15,14},{12,13},{1... | collective-permute-start | bytes 786440 | tf_op jit(solution)/shard_map/ppermute | solution.py:201
  18.3 7.7 %collective-permute-start.4 = (bf16[4,32,1024]{2,1,0:T(8,128)(2,1)S(1)}, bf16[4,32,1024]{2,1,0:T(8,128)(2,1)S(1)}, u32[]{:S(2)}, u32[]{:S(2)}) collective-permute-start(bf16[4,32,1024]{2,1,0:T(8,128)(2,1)S(1)} %pad_maximum_fusion), channel_id=1, source_target_pairs={{3,6},{7,10},{11,14},{15,12},{13,8},{9,4},{5,0},{6,3},{10,7},{14,1... | collective-permute-start | bytes 786440 | tf_op jit(solution)/shard_map/ppermute | solution.py:202
  30.1 6.1 %collective-permute-start.6 = (f32[2,2,1024]{2,1,0:T(2,128)S(1)}, f32[2,2,1024]{2,1,0:T(2,128)S(1)}, u32[]{:S(2)}, u32[]{:S(2)}) collective-permute-start(f32[2,2,1024]{2,1,0:T(2,128)S(1)} %get-tuple-element.19), channel_id=1, source_target_pairs={{2,2},{10,3},{6,6},{14,7},{3,10},{11,11},{7,14},{15,15},{13,4},{5,... | collective-permute-start | bytes 49160 | tf_op jit(solution)/shard_map/ppermute | solution.py:204
  32.5 4.7 %collective-permute-start.7 = (f32[2,2,1024]{2,1,0:T(2,128)S(1)}, f32[2,2,1024]{2,1,0:T(2,128)S(1)}, u32[]{:S(2)}, u32[]{:S(2)}) collective-permute-start(f32[2,2,1024]{2,1,0:T(2,128)S(1)} %get-tuple-element.20), channel_id=1, source_target_pairs={{3,2},{11,3},{7,6},{15,7},{2,10},{10,11},{6,14},{14,15},{12,4},{4,... | collective-permute-start | bytes 49160 | tf_op jit(solution)/shard_map/ppermute | solution.py:204
  32.6 5.1 %collective-permute-start.8 = (f32[2,2,1024]{2,1,0:T(2,128)S(1)}, f32[2,2,1024]{2,1,0:T(2,128)S(1)}, u32[]{:S(2)}, u32[]{:S(2)}) collective-permute-start(f32[2,2,1024]{2,1,0:T(2,128)S(1)} %get-tuple-element.21), channel_id=1, source_target_pairs={{6,2},{14,3},{2,6},{10,7},{7,10},{15,11},{3,14},{11,15},{9,4},{1,5... | collective-permute-start | bytes 49160 | tf_op jit(solution)/shard_map/ppermute | solution.py:204
  35.3 5.5 %collective-permute-start.9 = (f32[2,2,1024]{2,1,0:T(2,128)S(1)}, f32[2,2,1024]{2,1,0:T(2,128)S(1)}, u32[]{:S(2)}, u32[]{:S(2)}) collective-permute-start(f32[2,2,1024]{2,1,0:T(2,128)S(1)} %get-tuple-element.22), channel_id=1, source_target_pairs={{7,2},{15,3},{3,6},{11,7},{6,10},{14,11},{2,14},{10,15},{8,4},{0,5... | collective-permute-start | bytes 49160 | tf_op jit(solution)/shard_map/ppermute | solution.py:204

commit v3 on v2

--- a/solution.py
+++ b/solution.py
@@ -13,13 +13,12 @@
 VIEWS = 4
 ROUNDS = 2
 PAIRS = ROUNDS * VIEWS
-FLIP = 3
 PAD = (TILES - 1) * BX + LEVELS
 SCALE = 0.35 * math.log2(math.e)
 
 
 def slot_of(view, unit):
-    return 2 - view if (unit % 2 and view % 2 == 0) else view
+    return (view + 1) % VIEWS if unit % 2 else VIEWS - 1 - view
 
 
 def swap_bits(i):
@@ -40,7 +39,7 @@
             order = sorted(range(VIEWS), key=lambda v: slot_of(v, unit))
             for view in range(VIEWS):
                 for core in range(2):
-                    part = swap_bits(slot_of(view, unit)) ^ m ^ FLIP
+                    part = swap_bits(slot_of(view, unit)) ^ m
                     place = 4 * core + part
                     pairs.append((device(view, unit, core), device(order[place // 2], unit, place % 2)))
         share.append(pairs)
@@ -51,7 +50,18 @@
             line.append(device(order[place // 2], unit, place % 2))
     inner = [(line[i], line[i ^ 1]) for i in range(len(line))]
     outer = [(line[i], line[i + 1]) for i in range(1, len(line) - 1, 2)]
-    return share, inner, outer + [(j, i) for i, j in outer]
+    home = []
+    for e in range(2):
+        pairs = []
+        for unit in range(units):
+            order = sorted(range(VIEWS), key=lambda v: slot_of(v, unit))
+            for view in range(VIEWS):
+                for core in range(2):
+                    slot = slot_of(view, unit)
+                    sender = device(order[2 * core + (slot % 2 ^ e ^ 1)], unit, slot // 2)
+                    pairs.append((sender, device(view, unit, core)))
+        home.append(pairs)
+    return share, inner, outer + [(j, i) for i, j in outer], home
 
 
 def regress(scores, half, x_less_b):
@@ -102,23 +112,24 @@
             result, right, left = refs[VIEWS + 1 :]
         else:
             done = refs[VIEWS + 1]
-            outs = refs[VIEWS + 2 : 2 * VIEWS + 2]
-            right, left, result = refs[2 * VIEWS + 2 :]
+            outs = refs[VIEWS + 2 : VIEWS + 4]
+            right, left, result = refs[VIEWS + 4 :]
 
         place = numbers[3 * PAIRS]
         core = place % 2
 
-        def order_of(unit, rank):
-            return jnp.where((unit % 2 == 1) & (rank % 2 == 0), 2 - rank, rank)
+        def slot_in(unit, view):
+            return jnp.where(unit % 2 == 1, (view + 1) % VIEWS, VIEWS - 1 - view)
 
         def swap(i):
             return (i % 2) * 2 + i // 2
 
         def view_of(m):
-            return order_of(place // 8, swap((place % 4) ^ m ^ FLIP))
+            slot = swap((place % 4) ^ m)
+            return jnp.where(place // 8 % 2 == 1, (slot + VIEWS - 1) % VIEWS, VIEWS - 1 - slot)
 
         def buffer_of(view, place):
-            return (place % 4) ^ swap(order_of(place // 8, view)) ^ FLIP
+            return (place % 4) ^ swap(slot_in(place // 8, view))
 
         sender = place + 1 - 2 * core if inner else jnp.maximum(place - 1 + 2 * core, 0)
         middle = 1 - core if inner else core
@@ -142,7 +153,8 @@
             tile = numbers[2 * PAIRS + j]
             a, b = buffer_of(left_view, place), buffer_of(right_view, place)
             shift = (tile * BX).astype(jnp.float32)
-            home = ROUNDS * buffer_of(view, place) + j // VIEWS
+            there = slot_in(place // 8, view)
+            home = ROUNDS * (2 * ((there // 2) ^ core) + (there ^ (place % 8 // 2) ^ 1) % 2) + j // VIEWS
             for n in range(0, columns // BX, 2):
                 start = pl.multiple_of((TILES - 1 + n - tile) * BX, BX)
                 scores = jnp.dot(
@@ -156,11 +168,12 @@
 
         lax.fori_loop(0, PAIRS, one_pair, 0, unroll=4)
         if not inner:
-            for m in range(VIEWS):
-                for q in range(ROUNDS):
-                    both = [done[ROUNDS * m + q], result[ROUNDS * m + q]]
-                    outs[m][q, 0:1, :] = jnp.where(core == 0, both[1], both[0])
-                    outs[m][q, 1:2, :] = jnp.where(core == 0, both[0], both[1])
+            for i in range(2):
+                for e in range(2):
+                    for q in range(ROUNDS):
+                        at = ROUNDS * (2 * i + e) + q
+                        outs[i][e, q, 0:1, :] = jnp.where(core == 0, result[at], done[at])
+                        outs[i][e, q, 1:2, :] = jnp.where(core == 0, done[at], result[at])
 
     vmem = pl.BlockSpec(memory_space=pltpu.VMEM)
     operands = list(base) + [rim] + ([] if inner else [done])
@@ -168,9 +181,9 @@
     scratch = [pltpu.VMEM((VIEWS, PAD + columns, depth), jnp.bfloat16), pltpu.VMEM((VIEWS, depth, columns), jnp.bfloat16)]
     return pl.pallas_call(
         body,
-        out_shape=every if inner else [jax.ShapeDtypeStruct((ROUNDS, 2, columns), jnp.float32)] * VIEWS,
+        out_shape=every if inner else [jax.ShapeDtypeStruct((2, ROUNDS, 2, columns), jnp.float32)] * 2,
         in_specs=[pl.BlockSpec(memory_space=pltpu.SMEM)] + [vmem] * len(operands),
-        out_specs=vmem if inner else [vmem] * VIEWS,
+        out_specs=vmem if inner else [vmem] * 2,
         scratch_shapes=scratch if inner else scratch + [pltpu.VMEM(every.shape, every.dtype)],
         compiler_params=pltpu.CompilerParams(vmem_limit_bytes=48 << 20),
         name="band_inner" if inner else "band_outer",
@@ -181,12 +194,12 @@
     row_count = features.shape[0]
     strips = lax.axis_size("strip")
     per_view = strips // VIEWS
-    share, siblings, neighbours = tables(strips)
+    share, siblings, neighbours, home = tables(strips)
     index = (lax.axis_index("strip") - per_view // 2) % strips
     view, spot = index // per_view, index % per_view
     unit, core = spot // 2, spot % 2
-    slot = jnp.where((unit % 2 == 1) & (view % 2 == 0), 2 - view, view)
-    first = ((slot % 2) * 2 + slot // 2) ^ FLIP
+    slot = jnp.where(unit % 2 == 1, (view + 1) % VIEWS, VIEWS - 1 - view)
+    first = (slot % 2) * 2 + slot // 2
     place = 8 * unit + 2 * slot + core
     numbers = jnp.concatenate(
         [left_views.reshape(-1), right_step.reshape(-1), offset_tile.reshape(-1), place.astype(jnp.int32).reshape(1)]
@@ -200,11 +213,11 @@
     rows = [jnp.concatenate([lax.dynamic_slice_in_dim(g, r, 1, 0) for g in base], 0) for r in (1 - core, core)]
     beside = lax.ppermute(rows[0], "strip", siblings)
     beyond = lax.ppermute(rows[1], "strip", neighbours)
-    sent = band(numbers, base, beyond, band(numbers, base, beside, None))
-    back = [lax.ppermute(sent[m], "strip", [(j, i) for i, j in share[m]]) for m in range(VIEWS)]
-    back = [jnp.where(first % 2 == 1, back[m ^ 1], back[m]) for m in range(VIEWS)]
-    back = [jnp.where(first // 2 == 1, back[m ^ 2], back[m]) for m in range(VIEWS)]
-    return jnp.concatenate(back, 1)
+    kept, given = band(numbers, base, beyond, band(numbers, base, beside, None))
+    taken = lax.ppermute(given, "strip", siblings)
+    sent = jnp.where(core == 0, jnp.concatenate([kept, taken], 2), jnp.concatenate([taken, kept], 2))
+    back = [lax.ppermute(sent[e], "strip", home[e]) for e in range(2)]
+    return jnp.where(slot % 2 == 0, jnp.concatenate(back[::-1], 1), jnp.concatenate(back, 1))
 
 
 def solution(mesh):

time: 41.8 us -> 40.5 us (0.969)
  the two profiles are of different devices: /device:TPU:0 before, /device:TPU:1 now
where the time goes in v3:
time: 40.5 us; the launch traced here: 40.2 us
  starting transfers between devices  14.2 us (35%)
  waiting for transfers between devices  12.6 us (31%)
  Pallas kernels  8.3 us (20%)
  local copies, waits for them, and re-layouts  2.22 us (5%)
  other arithmetic  2.02 us (5%)
  between operations  0.82 us (2%)
    pallas_call x2, Pallas kernels, band(): pl.pallas_call(body, out_shape=every if inner else [jax.ShapeDtypeStruct(...  8.3 us
    ppermute x4, starting transfers between devices, per_device(): lax.ppermute(lax.dynamic_slice_in_dim(masked, 2 * (first ^ m), 2, 0), 'st...  7.65 us
    ppermute x4, waiting for transfers between devices, per_device(): lax.ppermute(lax.dynamic_slice_in_dim(masked, 2 * (first ^ m), 2, 0), 'st...  6.8 us
    ppermute x2, starting transfers between devices, per_device(): back = [lax.ppermute(sent[e], 'strip', home[e]) for e in range(2)]  4.11 us
    ppermute x2, waiting for transfers between devices, per_device(): back = [lax.ppermute(sent[e], 'strip', home[e]) for e in range(2)]  3.26 us
    ppermute x1, starting transfers between devices, per_device(): beyond = lax.ppermute(rows[1], 'strip', neighbours)  1.92 us
    unnamed x6, local copies, waits for them, and re-layouts  1.87 us
    ppermute x1, waiting for transfers between devices, per_device(): beyond = lax.ppermute(rows[1], 'strip', neighbours)  1.72 us
  transfers between devices with their start and end apart: 9, of which 6 were waited for; matrix products, arithmetic and copies ran while one was open for 1% of the time, Pallas kernels for 10%

profile of v3, /device:TPU:1, one launch (start us, length us, event | category | flops | bytes accessed | tf_op | source)
XLA Modules:
  0.0 40.2 jit_solution(18071106398808276909)
XLA Ops:
  0.7 1.1 %broadcast_select_fusion = bf16[8,32,1024]{2,1,0:T(8,128)(2,1)S(1)} fusion(bf16[8,32,1024]{2,1,0:T(8,128)(2,1)} %param.5, pred[8]{0:T(512)(128)(4,1)S(1)} %iota_compare_fusion), kind=kLoop, calls=%fused_computation | loop fusion | flops 262144 | bytes 1048584 | tf_op jit(solution)/shard_map/jit(_where)/select_n | solution.py:208
  1.9 4.2 %collective-permute-start.3 = (bf16[2,32,1024]{2,1,0:T(8,128)(2,1)S(1)}, bf16[2,32,1024]{2,1,0:T(8,128)(2,1)S(1)}, u32[]{:S(2)}, u32[]{:S(2)}) collective-permute-start(bf16[2,32,1024]{2,1,0:T(8,128)(2,1)S(1)} %get-tuple-element.19), channel_id=1, source_target_pairs={{2,14},{3,6},{6,10},{7,2},{10,15},{11,7},{14,11},{15,3},{4,1},{5,9... | collective-permute-start | bytes 393224 | tf_op jit(solution)/shard_map/ppermute | solution.py:211
  6.1 0.6 %collective-permute-start.2 = (bf16[2,32,1024]{2,1,0:T(8,128)(2,1)S(1)}, bf16[2,32,1024]{2,1,0:T(8,128)(2,1)S(1)}, u32[]{:S(2)}, u32[]{:S(2)}) collective-permute-start(bf16[2,32,1024]{2,1,0:T(8,128)(2,1)S(1)} %get-tuple-element.20), channel_id=1, source_target_pairs={{2,15},{3,7},{6,11},{7,3},{10,14},{11,6},{14,10},{15,2},{4,0},{5,8... | collective-permute-start | bytes 393224 | tf_op jit(solution)/shard_map/ppermute | solution.py:211
  6.8 0.4 collective-permute-start.1
  7.1 2.4 %collective-permute-start = (bf16[2,32,1024]{2,1,0:T(8,128)(2,1)S(1)}, bf16[2,32,1024]{2,1,0:T(8,128)(2,1)S(1)}, u32[]{:S(2)}, u32[]{:S(2)}) collective-permute-start(bf16[2,32,1024]{2,1,0:T(8,128)(2,1)S(1)} %get-tuple-element.22), channel_id=1, source_target_pairs={{2,11},{3,3},{6,15},{7,7},{10,10},{11,2},{14,14},{15,6},{4,4},{5,1... | collective-permute-start | bytes 393224 | tf_op jit(solution)/shard_map/ppermute | solution.py:211
  9.6 0.7 %copy-done = s32[2,4]{1,0:T(2,128)S(1)} copy-done((s32[2,4]{1,0:T(2,128)S(1)}, s32[2,4]{1,0:T(2,128)}, u32[]{:S(2)}) %copy-start) | copy-done | bytes 56
  10.3 0.1 reshape.19
  10.4 0.6 %copy-done.1 = s32[2,4]{1,0:T(2,128)S(1)} copy-done((s32[2,4]{1,0:T(2,128)S(1)}, s32[2,4]{1,0:T(2,128)}, u32[]{:S(2)}) %copy-start.1) | copy-done | bytes 56
  11.0 0.1 reshape.20
  11.0 0.6 %copy-done.2 = s32[2,4]{1,0:T(2,128)S(1)} copy-done((s32[2,4]{1,0:T(2,128)S(1)}, s32[2,4]{1,0:T(2,128)}, u32[]{:S(2)}) %copy-start.2) | copy-done | bytes 56
  11.6 0.1 reshape.21
  11.8 1.7 %collective-permute-done.2.refs_2_ = bf16[2,32,1024]{2,1,0:T(8,128)(2,1)S(1)} collective-permute-done((bf16[2,32,1024]{2,1,0:T(8,128)(2,1)S(1)}, bf16[2,32,1024]{2,1,0:T(8,128)(2,1)S(1)}, u32[]{:S(2)}, u32[]{:S(2)}) %collective-permute-start.2) | collective-permute-done | bytes 131104 | tf_op jit(solution)/shard_map/ppermute | solution.py:211
  13.5 5.1 %collective-permute-done.refs_0_ = bf16[2,32,1024]{2,1,0:T(8,128)(2,1)S(1)} collective-permute-done((bf16[2,32,1024]{2,1,0:T(8,128)(2,1)S(1)}, bf16[2,32,1024]{2,1,0:T(8,128)(2,1)S(1)}, u32[]{:S(2)}, u32[]{:S(2)}) %collective-permute-start) | collective-permute-done | bytes 131104 | tf_op jit(solution)/shard_map/ppermute | solution.py:211
  18.8 1.9 %collective-permute-start.4 = (bf16[4,32,1024]{2,1,0:T(8,128)(2,1)S(1)}, bf16[4,32,1024]{2,1,0:T(8,128)(2,1)S(1)}, u32[]{:S(2)}, u32[]{:S(2)}) collective-permute-start(bf16[4,32,1024]{2,1,0:T(8,128)(2,1)S(1)} %pad_maximum_fusion), channel_id=1, source_target_pairs={{15,10},{11,6},{7,2},{3,0},{1,4},{5,8},{9,12},{10,15},{6,11},{2,7}... | collective-permute-start | bytes 786440 | tf_op jit(solution)/shard_map/ppermute | solution.py:215
  20.8 4.1 %band_inner.1.refs_5_ = f32[8,1,1024]{2,1,0:T(1,128)S(1)} custom-call(s32[25]{0:T(128)S(1)} %pad_add_fusion.numbers, bf16[2,32,1024]{2,1,0:T(8,128)(2,1)S(1)} %collective-permute-done.refs_0_, bf16[2,32,1024]{2,1,0:T(8,128)(2,1)S(1)} %collective-permute-done.1.refs_1_, bf16[2,32,1024]{2,1,0:T(8,128)(2,1)S(1)} %collective-permute-done.2.refs_2_, ...), custom_call_target="tpu_custom_call" | custom-call | tf_op jit(solution)/shard_map/band_inner/pallas_call | solution.py:182
  24.9 1.7 %collective-permute-done.4.refs_4_ = bf16[4,32,1024]{2,1,0:T(8,128)(2,1)S(1)} collective-permute-done((bf16[4,32,1024]{2,1,0:T(8,128)(2,1)S(1)}, bf16[4,32,1024]{2,1,0:T(8,128)(2,1)S(1)}, u32[]{:S(2)}, u32[]{:S(2)}) %collective-permute-start.4) | collective-permute-done | bytes 262176 | tf_op jit(solution)/shard_map/ppermute | solution.py:215
  26.6 4.2 %band_outer.1 = (f32[2,2,2,1024]{3,2,1,0:T(2,128)S(1)}, f32[2,2,2,1024]{3,2,1,0:T(2,128)S(1)}) custom-call(s32[25]{0:T(128)S(1)} %pad_add_fusion.numbers, bf16[2,32,1024]{2,1,0:T(8,128)(2,1)S(1)} %collective-permute-done.refs_0_, bf16[2,32,1024]{2,1,0:T(8,128)(2,1)S(1)} %collective-permute-done.1.refs_1_, ...), custom_call_target="tpu_custom_call" | custom-call | tf_op jit(solution)/shard_map/band_outer/pallas_call | solution.py:182
  30.8 0.5 %collective-permute-start.6 = (f32[2,2,2,1024]{3,2,1,0:T(2,128)S(1)}, f32[2,2,2,1024]{3,2,1,0:T(2,128)S(1)}, u32[]{:S(2)}, u32[]{:S(2)}) collective-permute-start(f32[2,2,2,1024]{3,2,1,0:T(2,128)S(1)} %get-tuple-element.18), channel_id=1, source_target_pairs={{14,15},{15,14},{10,11},{11,10},{6,7},{7,6},{2,3},{3,2},{0,1},{1,0... | collective-permute-start | bytes 98312 | tf_op jit(solution)/shard_map/ppermute | solution.py:217
  31.2 0.9 %collective-permute-done.6 = f32[2,2,2,1024]{3,2,1,0:T(2,128)S(1)} collective-permute-done((f32[2,2,2,1024]{3,2,1,0:T(2,128)S(1)}, f32[2,2,2,1024]{3,2,1,0:T(2,128)S(1)}, u32[]{:S(2)}, u32[]{:S(2)}) %collective-permute-start.6) | collective-permute-done | bytes 32800 | tf_op jit(solution)/shard_map/ppermute | solution.py:217
  32.2 2.2 %collective-permute-start.7 = (f32[2,4,1024]{2,1,0:T(4,128)S(1)}, f32[2,4,1024]{2,1,0:T(4,128)S(1)}, u32[]{:S(2)}, u32[]{:S(2)}) collective-permute-start(f32[2,4,1024]{2,1,0:T(4,128)S(1)} %get-tuple-element.31), channel_id=1, source_target_pairs={{11,2},{3,3},{15,6},{7,7},{10,10},{2,11},{14,14},{6,15},{4,4},{12,... | collective-permute-start | bytes 98312 | tf_op jit(solution)/shard_map/ppermute | solution.py:219
  34.3 1.9 %collective-permute-start.8 = (f32[2,4,1024]{2,1,0:T(4,128)S(1)}, f32[2,4,1024]{2,1,0:T(4,128)S(1)}, u32[]{:S(2)}, u32[]{:S(2)}) collective-permute-start(f32[2,4,1024]{2,1,0:T(4,128)S(1)} %get-tuple-element.32), channel_id=1, source_target_pairs={{15,2},{7,3},{11,6},{3,7},{14,10},{6,11},{10,14},{2,15},{0,4},{8,5... | collective-permute-start | bytes 98312 | tf_op jit(solution)/shard_map/ppermute | solution.py:219
  36.3 2.0 %collective-permute-done.7 = f32[2,4,1024]{2,1,0:T(4,128)S(1)} collective-permute-done((f32[2,4,1024]{2,1,0:T(4,128)S(1)}, f32[2,4,1024]{2,1,0:T(4,128)S(1)}, u32[]{:S(2)}, u32[]{:S(2)}) %collective-permute-start.7) | collective-permute-done | bytes 32800 | tf_op jit(solution)/shard_map/ppermute | solution.py:219
  38.3 1.2 %collective-permute-done.8 = f32[2,4,1024]{2,1,0:T(4,128)S(1)} collective-permute-done((f32[2,4,1024]{2,1,0:T(4,128)S(1)}, f32[2,4,1024]{2,1,0:T(4,128)S(1)}, u32[]{:S(2)}, u32[]{:S(2)}) %collective-permute-start.8) | collective-permute-done | bytes 32800 | tf_op jit(solution)/shard_map/ppermute | solution.py:219
  39.5 0.7 %maximum_select_fusion.1 = f32[2,8,1024]{2,1,0:T(8,128)} fusion(f32[2,4,1024]{2,1,0:T(4,128)S(1)} %collective-permute-done.8, f32[2,4,1024]{2,1,0:T(4,128)S(1)} %collective-permute-done.7, pred[]{:T(512)S(6)} %eq.18), kind=kLoop, calls=%fused_computation.4 | loop fusion | flops 49152 | bytes 131073 | tf_op jit(solution)/shard_map/jit(_where)/select_n | solution.py:220
  (16 shorter events, 0.4 us)
Async XLA Ops:
  1.9 9.9 %collective-permute-start.3 = (bf16[2,32,1024]{2,1,0:T(8,128)(2,1)S(1)}, bf16[2,32,1024]{2,1,0:T(8,128)(2,1)S(1)}, u32[]{:S(2)}, u32[]{:S(2)}) collective-permute-start(bf16[2,32,1024]{2,1,0:T(8,128)(2,1)S(1)} %get-tuple-element.19), channel_id=1, source_target_pairs={{2,14},{3,6},{6,10},{7,2},{10,15},{11,7},{14,11},{15,3},{4,1},{5,9... | collective-permute-start | bytes 393224 | tf_op jit(solution)/shard_map/ppermute | solution.py:211
  6.1 7.4 %collective-permute-start.2 = (bf16[2,32,1024]{2,1,0:T(8,128)(2,1)S(1)}, bf16[2,32,1024]{2,1,0:T(8,128)(2,1)S(1)}, u32[]{:S(2)}, u32[]{:S(2)}) collective-permute-start(bf16[2,32,1024]{2,1,0:T(8,128)(2,1)S(1)} %get-tuple-element.20), channel_id=1, source_target_pairs={{2,15},{3,7},{6,11},{7,3},{10,14},{11,6},{14,10},{15,2},{4,0},{5,8... | collective-permute-start | bytes 393224 | tf_op jit(solution)/shard_map/ppermute | solution.py:211
  6.8 6.8 %collective-permute-start.1 = (bf16[2,32,1024]{2,1,0:T(8,128)(2,1)S(1)}, bf16[2,32,1024]{2,1,0:T(8,128)(2,1)S(1)}, u32[]{:S(2)}, u32[]{:S(2)}) collective-permute-start(bf16[2,32,1024]{2,1,0:T(8,128)(2,1)S(1)} %get-tuple-element.21), channel_id=1, source_target_pairs={{2,10},{3,2},{6,14},{7,6},{10,11},{11,3},{14,15},{15,7},{4,5},{5,1... | collective-permute-start | bytes 393224 | tf_op jit(solution)/shard_map/ppermute | solution.py:211
  7.1 11.5 %collective-permute-start = (bf16[2,32,1024]{2,1,0:T(8,128)(2,1)S(1)}, bf16[2,32,1024]{2,1,0:T(8,128)(2,1)S(1)}, u32[]{:S(2)}, u32[]{:S(2)}) collective-permute-start(bf16[2,32,1024]{2,1,0:T(8,128)(2,1)S(1)} %get-tuple-element.22), channel_id=1, source_target_pairs={{2,11},{3,3},{6,15},{7,7},{10,10},{11,2},{14,14},{15,6},{4,4},{5,1... | collective-permute-start | bytes 393224 | tf_op jit(solution)/shard_map/ppermute | solution.py:211
  9.6 0.7 %copy-start = (s32[2,4]{1,0:T(2,128)S(1)}, s32[2,4]{1,0:T(2,128)}, u32[]{:S(2)}) copy-start(s32[2,4]{1,0:T(2,128)} %param.7) | copy-start | bytes 100
  10.3 0.7 %copy-start.1 = (s32[2,4]{1,0:T(2,128)S(1)}, s32[2,4]{1,0:T(2,128)}, u32[]{:S(2)}) copy-start(s32[2,4]{1,0:T(2,128)} %param.8) | copy-start | bytes 100
  10.9 0.7 %copy-start.2 = (s32[2,4]{1,0:T(2,128)S(1)}, s32[2,4]{1,0:T(2,128)}, u32[]{:S(2)}) copy-start(s32[2,4]{1,0:T(2,128)} %param.9) | copy-start | bytes 100
  18.7 2.1 %collective-permute-start.5 = (bf16[4,32,1024]{2,1,0:T(8,128)(2,1)S(1)}, bf16[4,32,1024]{2,1,0:T(8,128)(2,1)S(1)}, u32[]{:S(2)}, u32[]{:S(2)}) collective-permute-start(bf16[4,32,1024]{2,1,0:T(8,128)(2,1)S(1)} %pad_maximum_fusion.1), channel_id=1, source_target_pairs={{14,15},{15,14},{10,11},{11,10},{6,7},{7,6},{2,3},{3,2},{0,1},{1,0... | collective-permute-start | bytes 786440 | tf_op jit(solution)/shard_map/ppermute | solution.py:214
  18.8 7.8 %collective-permute-start.4 = (bf16[4,32,1024]{2,1,0:T(8,128)(2,1)S(1)}, bf16[4,32,1024]{2,1,0:T(8,128)(2,1)S(1)}, u32[]{:S(2)}, u32[]{:S(2)}) collective-permute-start(bf16[4,32,1024]{2,1,0:T(8,128)(2,1)S(1)} %pad_maximum_fusion), channel_id=1, source_target_pairs={{15,10},{11,6},{7,2},{3,0},{1,4},{5,8},{9,12},{10,15},{6,11},{2,7}... | collective-permute-start | bytes 786440 | tf_op jit(solution)/shard_map/ppermute | solution.py:215
  30.8 1.3 %collective-permute-start.6 = (f32[2,2,2,1024]{3,2,1,0:T(2,128)S(1)}, f32[2,2,2,1024]{3,2,1,0:T(2,128)S(1)}, u32[]{:S(2)}, u32[]{:S(2)}) collective-permute-start(f32[2,2,2,1024]{3,2,1,0:T(2,128)S(1)} %get-tuple-element.18), channel_id=1, source_target_pairs={{14,15},{15,14},{10,11},{11,10},{6,7},{7,6},{2,3},{3,2},{0,1},{1,0... | collective-permute-start | bytes 98312 | tf_op jit(solution)/shard_map/ppermute | solution.py:217
  32.2 6.1 %collective-permute-start.7 = (f32[2,4,1024]{2,1,0:T(4,128)S(1)}, f32[2,4,1024]{2,1,0:T(4,128)S(1)}, u32[]{:S(2)}, u32[]{:S(2)}) collective-permute-start(f32[2,4,1024]{2,1,0:T(4,128)S(1)} %get-tuple-element.31), channel_id=1, source_target_pairs={{11,2},{3,3},{15,6},{7,7},{10,10},{2,11},{14,14},{6,15},{4,4},{12,... | collective-permute-start | bytes 98312 | tf_op jit(solution)/shard_map/ppermute | solution.py:219
  34.3 5.2 %collective-permute-start.8 = (f32[2,4,1024]{2,1,0:T(4,128)S(1)}, f32[2,4,1024]{2,1,0:T(4,128)S(1)}, u32[]{:S(2)}, u32[]{:S(2)}) collective-permute-start(f32[2,4,1024]{2,1,0:T(4,128)S(1)} %get-tuple-element.32), channel_id=1, source_target_pairs={{15,2},{7,3},{11,6},{3,7},{14,10},{6,11},{10,14},{2,15},{0,4},{8,5... | collective-permute-start | bytes 98312 | tf_op jit(solution)/shard_map/ppermute | solution.py:219

commit v4 on v3

v4 whole, which is shorter than its diff:
```python
import functools
import math

import jax
import jax.numpy as jnp
from jax import lax
from jax.experimental import pallas as pl
from jax.experimental.pallas import tpu as pltpu
from jax.sharding import PartitionSpec as P

LEVELS = 256
BX = 128
TILES = 4
VIEWS = 4
ROUNDS = 2
PAIRS = ROUNDS * VIEWS
UNROLL = 4
PAD = (TILES - 1) * BX + LEVELS
SCALE = 0.35 * math.log2(math.e)


def slot_of(view, unit):
    return (view + 1) % VIEWS if unit % 2 else VIEWS - 1 - view


def swap_bits(i):
    return ((i & 1) << 1) | (i >> 1)


def tables(strips):
    per_view = strips // VIEWS

    def device(view, unit, core):
        return (view * per_view + 2 * unit + core + per_view // 2) % strips

    units = per_view // 2
    share = []
    for m in range(VIEWS):
        pairs = []
        for unit in range(units):
            order = sorted(range(VIEWS), key=lambda v: slot_of(v, unit))
            for view in range(VIEWS):
                for core in range(2):
                    slot, here = slot_of(view, unit), device(view, unit, core)
                    place = 4 * core + (swap_bits(slot) ^ m)
                    there = device(order[place // 2], unit, place % 2)
                    pairs.append((here, device(order[slot ^ 1], unit, core) if there == here else there))
        share.append(pairs)
    line = []
    for unit in range(units):
        order = sorted(range(VIEWS), key=lambda v: slot_of(v, unit))
        for place in range(8):
            line.append(device(order[place // 2], unit, place % 2))
    inner = [(line[i], line[i ^ 1]) for i in range(len(line))]
    outer = [(line[i], line[(i + 1) % len(line)]) for i in range(1, len(line), 2)]
    home = []
    for e in range(2):
        pairs = []
        for unit in range(units):
            order = sorted(range(VIEWS), key=lambda v: slot_of(v, unit))
            for view in range(VIEWS):
                for core in range(2):
                    slot = slot_of(view, unit)
                    sender, here = device(order[2 * core + (slot % 2 ^ e ^ 1)], unit, slot // 2), device(view, unit, core)
                    pairs.append((device(order[slot ^ 1], unit, core) if sender == here else sender, here))
        home.append(pairs)
    return share, inner, outer + [(j, i) for i, j in outer], home


def regress(scores, half, x_less_b):
    groups = BX // 8

    def part(span, a):
        first = (span + half) * BX + 8 * a
        return scores[first : first + 8, half * BX : (half + 1) * BX]

    near = [jnp.where(x_less_b < 8 * a, part(0, a), part(2, a)) for a in range(groups)]
    far = [part(1, a) for a in range(groups)]
    tops = [functools.reduce(jnp.maximum, near), functools.reduce(jnp.maximum, far)]
    top = jnp.broadcast_to(jnp.max(jnp.maximum(*tops), axis=0, keepdims=True), (8, BX))

    def weight(value):
        return jnp.exp2((value - top) * SCALE)

    total = moment = weight(far[-1])
    for value in far[-2::-1]:
        total = total + weight(value)
        moment = moment + total
    wrapped = total
    for a in range(groups - 1, -1, -1):
        total = total + weight(near[a])
        wrapped = jnp.where(x_less_b < 8 * a, total, wrapped)
        if a:
            moment = moment + total
    moment = x_less_b.astype(jnp.float32) * total - 8.0 * moment + 256.0 * wrapped
    return jnp.sum(moment, axis=0, keepdims=True) / jnp.sum(total, axis=0, keepdims=True)


class Place:
    def __init__(self, place):
        self.place = place
        self.unit, self.slot, self.core = place // 8, place % 8 // 2, place % 2

    def slot_of(self, view):
        return jnp.where(self.unit % 2 == 1, (view + 1) % VIEWS, VIEWS - 1 - view)

    def view_at(self, slot):
        return jnp.where(self.unit % 2 == 1, (slot + VIEWS - 1) % VIEWS, VIEWS - 1 - slot)

    def view_of(self, buffer):
        return self.view_at(swap_bits((self.place % 4) ^ buffer))

    def buffer_of(self, view):
        return (self.place % 4) ^ swap_bits(self.slot_of(view))

    def view_home(self, group, e):
        return self.view_at(2 * (self.core ^ group) + (e ^ 1 ^ (self.slot % 2)))


def correlate(numbers, at, right, left, result, groups):
    columns = result.shape[-1]
    x_less_b = lax.broadcasted_iota(jnp.int32, (8, BX), 1) - lax.broadcasted_iota(jnp.int32, (8, BX), 0)

    def one_pair(i, carry):
        q, e, group = i % 2, i // 2 % 2, i // 4
        j = VIEWS * q + at.view_home(group, e)
        left_view = numbers[j]
        right_view = (left_view + numbers[PAIRS + j]) % VIEWS
        tile = numbers[2 * PAIRS + j]
        a, b = at.buffer_of(left_view), at.buffer_of(right_view)
        shift = (tile * BX).astype(jnp.float32)
        for n in range(0, columns // BX, 2):
            start = pl.multiple_of((TILES - 1 + n - tile) * BX, BX)
            scores = jnp.dot(
                right[b, pl.ds(start, 2 * BX + LEVELS), :],
                left[a, :, n * BX : (n + 2) * BX],
                preferred_element_type=jnp.float32,
            )
            for k in range(2):
                result[i, :, (n + k) * BX : (n + k + 1) * BX] = regress(scores, k, x_less_b) + shift
        return carry

    lax.fori_loop(4 * groups[0], 4 * groups[-1] + 4, one_pair, 0, unroll=UNROLL)


def shares_of(middle, channels):
    heavy = 0.25 + 0.25 * middle.astype(jnp.float32)
    return [jnp.full((channels, BX), w).astype(jnp.bfloat16) for w in (0.75 - heavy, heavy)]


def band_inner(numbers, base, rim):
    _, channels, columns = base[0].shape
    depth = 4 * channels

    def body(numbers, *refs):
        base, (rim, result, right, outer_left, left) = refs[:VIEWS], refs[VIEWS:]
        at = Place(numbers[3 * PAIRS])
        beside = Place(at.place + 1 - 2 * at.core)
        inner, outer = shares_of(1 - at.core, channels), shares_of(at.core, channels)
        nothing = jnp.zeros((channels, BX), jnp.bfloat16)
        for m in range(VIEWS):
            there = beside.buffer_of(at.view_of(m))
            right[m, :PAD, :] = jnp.zeros((PAD, depth), jnp.bfloat16)
            for n in range(columns // BX):
                span = slice(n * BX, (n + 1) * BX)
                pair = [base[m][0, :, span], base[m][1, :, span]]
                third = rim[there, :, span]
                right[m, PAD + n * BX : PAD + (n + 1) * BX, :] = jnp.concatenate([third] + pair + [nothing], 0).T
                mixed = [r * w for r, w in zip(pair, inner)]
                left[m, :, span] = jnp.concatenate([third * jnp.bfloat16(0.25)] + mixed + [nothing], 0)
                mixed = [r * w for r, w in zip(pair, outer)]
                outer_left[m, channels:, span] = jnp.concatenate(mixed + [nothing], 0)
        correlate(numbers, at, right, left, result, (0, 1))

    vmem = pl.BlockSpec(memory_space=pltpu.VMEM)
    return pl.pallas_call(
        body,
        out_shape=[
            jax.ShapeDtypeStruct((PAIRS, 1, columns), jnp.float32),
            jax.ShapeDtypeStruct((VIEWS, PAD + columns, depth), jnp.bfloat16),
            jax.ShapeDtypeStruct((VIEWS, depth, columns), jnp.bfloat16),
        ],
        in_specs=[pl.BlockSpec(memory_space=pltpu.SMEM)] + [vmem] * (VIEWS + 1),
        out_specs=[vmem] * 3,
        scratch_shapes=[pltpu.VMEM((VIEWS, depth, columns), jnp.bfloat16)],
        compiler_params=pltpu.CompilerParams(vmem_limit_bytes=48 << 20),
        name="band_inner",
    )(numbers, *base, rim)


def both_rows(core, first, second, group, out):
    for e in range(2):
        for q in range(ROUNDS):
            i = 4 * group + 2 * e + q
            out[e, q, 0:1, :] = jnp.where(core == 0, first[i], second[i])
            out[e, q, 1:2, :] = jnp.where(core == 0, second[i], first[i])


def band_given(numbers, rim, done, right, left, places):
    _, channels, columns = rim.shape

    def body(numbers, rim, done, right_in, left_in, given, right, left, result):
        at = Place(numbers[3 * PAIRS])
        beyond = Place((at.place - 1 + 2 * at.core + places) % places)
        edge = at.place == jnp.where(at.core == 0, 0, places - 1)
        share = jnp.full((channels, BX), jnp.where(edge, 0.0, 0.25)).astype(jnp.bfloat16)
        for m in range(VIEWS):
            there = beyond.buffer_of(at.view_of(m))
            for n in range(columns // BX):
                span = slice(n * BX, (n + 1) * BX)
                third = rim[there, :, span]
                right[m, PAD + n * BX : PAD + (n + 1) * BX, :channels] = third.T
                left[m, :channels, span] = third * share
        correlate(numbers, at, right, left, result, (1,))
        both_rows(at.core, result, done, 1, given)

    vmem = pl.BlockSpec(memory_space=pltpu.VMEM)
    return pl.pallas_call(
        body,
        out_shape=[
            jax.ShapeDtypeStruct((2, ROUNDS, 2, columns), jnp.float32),
            jax.ShapeDtypeStruct(right.shape, right.dtype),
            jax.ShapeDtypeStruct(left.shape, left.dtype),
        ],
        in_specs=[pl.BlockSpec(memory_space=pltpu.SMEM)] + [vmem] * 4,
        out_specs=[vmem] * 3,
        input_output_aliases={3: 1, 4: 2},
        scratch_shapes=[pltpu.VMEM(done.shape, done.dtype)],
        compiler_params=pltpu.CompilerParams(vmem_limit_bytes=48 << 20),
        name="band_given",
    )(numbers, rim, done, right, left)


def band_kept(numbers, done, right, left):
    columns = done.shape[-1]

    def body(numbers, done, right, left, kept, result):
        at = Place(numbers[3 * PAIRS])
        correlate(numbers, at, right, left, result, (0,))
        both_rows(at.core, result, done, 0, kept)

    vmem = pl.BlockSpec(memory_space=pltpu.VMEM)
    return pl.pallas_call(
        body,
        out_shape=jax.ShapeDtypeStruct((2, ROUNDS, 2, columns), jnp.float32),
        in_specs=[pl.BlockSpec(memory_space=pltpu.SMEM)] + [vmem] * 3,
        out_specs=vmem,
        scratch_shapes=[pltpu.VMEM(done.shape, done.dtype)],
        compiler_params=pltpu.CompilerParams(vmem_limit_bytes=48 << 20),
        name="band_kept",
    )(numbers, done, right, left)


def per_device(features, valid_rows, left_views, right_step, offset_tile):
    row_count = features.shape[0]
    strips = lax.axis_size("strip")
    per_view = strips // VIEWS
    share, siblings, neighbours, home = tables(strips)
    index = (lax.axis_index("strip") - per_view // 2) % strips
    view, spot = index // per_view, index % per_view
    unit, core = spot // 2, spot % 2
    slot = jnp.where(unit % 2 == 1, (view + 1) % VIEWS, VIEWS - 1 - view)
    first = (slot % 2) * 2 + slot // 2
    place = 8 * unit + 2 * slot + core
    numbers = jnp.concatenate(
        [left_views.reshape(-1), right_step.reshape(-1), offset_tile.reshape(-1), place.astype(jnp.int32).reshape(1)]
    )
    row_ids = lax.broadcasted_iota(jnp.int32, (row_count, 1, 1), 0)
    masked = jnp.where(row_ids >= row_count - valid_rows[0], features, jnp.zeros_like(features))
    stays = slot // 2 == core
    pieces = [lax.dynamic_slice_in_dim(masked, 2 * (first ^ m), 2, 0) for m in range(VIEWS)]
    base = [lax.ppermute(pieces[m], "strip", share[m]) for m in range(VIEWS)]
    base[0] = jnp.where(stays, pieces[0], base[0])
    numbers, base = lax.optimization_barrier((numbers, base))
    rows = [jnp.concatenate([lax.dynamic_slice_in_dim(g, r, 1, 0) for g in base], 0) for r in (1 - core, core)]
    beside = lax.ppermute(rows[0], "strip", siblings)
    beyond = lax.ppermute(rows[1], "strip", neighbours)
    done, right, left = band_inner(numbers, base, beside)
    given, right, left = band_given(numbers, beyond, done, right, left, strips)
    taken = lax.ppermute(given, "strip", siblings)
    kept = band_kept(numbers, done, right, left)
    sent = jnp.where(core == 0, jnp.concatenate([kept, taken], 2), jnp.concatenate([taken, kept], 2))
    back = [lax.ppermute(sent[e], "strip", home[e]) for e in range(2)]
    back[1] = jnp.where(stays, sent[1], back[1])
    return jnp.where(slot % 2 == 0, jnp.concatenate(back[::-1], 1), jnp.concatenate(back, 1))


def solution(mesh):
    return jax.shard_map(
        per_device,
        mesh=mesh,
        in_specs=(
            P(("groups", "strip"), None, None),
            P(("groups", "strip")),
            P("groups", None),
            P("groups", None),
            P("groups", None),
        ),
        out_specs=P(None, ("groups", "strip"), None),
        check_vma=False,
    )
```

time: 40.5 us -> 37.5 us (0.926)
  local copies, waits for them, and re-layouts: 2.22 us -> 0.36 us
  starting transfers between devices: 14.2 us -> 13 us
    ppermute x1, starting transfers between devices: 0.07 us -> 3.28 us  [per_device(): beside = lax.ppermute(rows[0], 'strip', siblings)]
    unnamed x6, local copies, waits for them, and re-layouts: 1.87 us -> 0.01 us
    ppermute x1, starting transfers between devices: 1.92 us -> 0.18 us  [per_device(): beyond = lax.ppermute(rows[1], 'strip', neighbours)]
    ppermute x2, starting transfers between devices: 4.11 us -> 2.9 us  [per_device(): back = [lax.ppermute(sent[e], 'strip', home[e]) for e in range(2)]]
    ppermute x4, starting transfers between devices: 7.65 us -> 6.58 us  [per_device(): base = [lax.ppermute(pieces[m], 'strip', share[m]) for m in range(VIEWS)]]
    ppermute x1, waiting for transfers between devices: 1.72 us -> 0.75 us  [per_device(): beyond = lax.ppermute(rows[1], 'strip', neighbours)]
    ppermute x1, waiting for transfers between devices: 0.01 us -> 0.94 us  [per_device(): beside = lax.ppermute(rows[0], 'strip', siblings)]
    ppermute x1, waiting for transfers between devices: 0.86 us -> 0.01 us  [per_device(): taken = lax.ppermute(given, 'strip', siblings)]
  transfers between devices with their start and end apart: 9 -> 9, of which waited for: 6 -> 7; matrix products, arithmetic and copies ran while one was open for 1% -> 1% of each run, Pallas kernels for 10% -> 16%
where the time goes in v4:
time: 37.5 us; the launch traced here: 37.3 us
  starting transfers between devices  13 us (35%)
  waiting for transfers between devices  12.4 us (33%)
  Pallas kernels  8.63 us (23%)
  other arithmetic  2.04 us (5%)
  between operations  0.91 us (2%)
    ppermute x4, waiting for transfers between devices, per_device(): base = [lax.ppermute(pieces[m], 'strip', share[m]) for m in range(VIEWS)]  6.84 us
    ppermute x4, starting transfers between devices, per_device(): base = [lax.ppermute(pieces[m], 'strip', share[m]) for m in range(VIEWS)]  6.58 us
    pallas_call x1, Pallas kernels, band_inner(): pl.pallas_call(body, out_shape=[jax.ShapeDtypeStruct((PAIRS, 1, columns),...  3.98 us
    ppermute x2, waiting for transfers between devices, per_device(): back = [lax.ppermute(sent[e], 'strip', home[e]) for e in range(2)]  3.84 us
    ppermute x1, starting transfers between devices, per_device(): beside = lax.ppermute(rows[0], 'strip', siblings)  3.28 us
    ppermute x2, starting transfers between devices, per_device(): back = [lax.ppermute(sent[e], 'strip', home[e]) for e in range(2)]  2.9 us
    pallas_call x1, Pallas kernels, band_given(): pl.pallas_call(body, out_shape=[jax.ShapeDtypeStruct((2, ROUNDS, 2, colum...  2.64 us
    pallas_call x1, Pallas kernels, band_kept(): pl.pallas_call(body, out_shape=jax.ShapeDtypeStruct((2, ROUNDS, 2, column...  2.01 us
  transfers between devices with their start and end apart: 9, of which 7 were waited for; matrix products, arithmetic and copies ran while one was open for 1% of the time, Pallas kernels for 16%

profile of v4, /device:TPU:1, one launch (start us, length us, event | category | flops | bytes accessed | tf_op | source)
XLA Modules:
  0.0 37.3 jit_solution(12342920892110383986)
XLA Ops:
  0.8 1.1 %broadcast_select_fusion = bf16[8,32,1024]{2,1,0:T(8,128)(2,1)S(1)} fusion(bf16[8,32,1024]{2,1,0:T(8,128)(2,1)} %param.5, pred[8]{0:T(512)(128)(4,1)S(1)} %iota_compare_fusion), kind=kLoop, calls=%fused_computation | loop fusion | flops 262144 | bytes 1048584 | tf_op jit(solution)/shard_map/jit(_where)/select_n | solution.py:269
  2.1 3.8 %collective-permute-start = (bf16[2,32,1024]{2,1,0:T(8,128)(2,1)S(1)}, bf16[2,32,1024]{2,1,0:T(8,128)(2,1)S(1)}, u32[]{:S(2)}, u32[]{:S(2)}) collective-permute-start(bf16[2,32,1024]{2,1,0:T(8,128)(2,1)S(1)} %get-tuple-element.30), channel_id=1, source_target_pairs={{2,11},{3,7},{6,15},{7,3},{10,14},{11,2},{14,10},{15,6},{4,0},{5,1... | collective-permute-start | bytes 393224 | tf_op jit(solution)/shard_map/ppermute | solution.py:272
  5.8 0.6 %collective-permute-start.3 = (bf16[2,32,1024]{2,1,0:T(8,128)(2,1)S(1)}, bf16[2,32,1024]{2,1,0:T(8,128)(2,1)S(1)}, u32[]{:S(2)}, u32[]{:S(2)}) collective-permute-start(bf16[2,32,1024]{2,1,0:T(8,128)(2,1)S(1)} %get-tuple-element.27), channel_id=1, source_target_pairs={{2,14},{3,6},{6,10},{7,2},{10,15},{11,7},{14,11},{15,3},{4,1},{5,9... | collective-permute-start | bytes 393224 | tf_op jit(solution)/shard_map/ppermute | solution.py:272
  6.4 2.2 %collective-permute-start.2 = (bf16[2,32,1024]{2,1,0:T(8,128)(2,1)S(1)}, bf16[2,32,1024]{2,1,0:T(8,128)(2,1)S(1)}, u32[]{:S(2)}, u32[]{:S(2)}) collective-permute-start(bf16[2,32,1024]{2,1,0:T(8,128)(2,1)S(1)} %get-tuple-element.28), channel_id=1, source_target_pairs={{2,15},{3,7},{6,11},{7,3},{10,14},{11,6},{14,10},{15,2},{4,0},{5,8... | collective-permute-start | bytes 393224 | tf_op jit(solution)/shard_map/ppermute | solution.py:272
  8.6 0.1 reshape.19
  8.7 0.1 reshape.20
  8.8 0.1 reshape.21
  8.9 0.1 pad_add_fusion.numbers
  9.0 0.1 collective-permute-done
  9.1 2.8 %collective-permute-done.3.refs_3_ = bf16[2,32,1024]{2,1,0:T(8,128)(2,1)S(1)} collective-permute-done((bf16[2,32,1024]{2,1,0:T(8,128)(2,1)S(1)}, bf16[2,32,1024]{2,1,0:T(8,128)(2,1)S(1)}, u32[]{:S(2)}, u32[]{:S(2)}) %collective-permute-start.3) | collective-permute-done | bytes 131104 | tf_op jit(solution)/shard_map/ppermute | solution.py:272
  11.9 4.0 %collective-permute-done.2.refs_2_ = bf16[2,32,1024]{2,1,0:T(8,128)(2,1)S(1)} collective-permute-done((bf16[2,32,1024]{2,1,0:T(8,128)(2,1)S(1)}, bf16[2,32,1024]{2,1,0:T(8,128)(2,1)S(1)}, u32[]{:S(2)}, u32[]{:S(2)}) %collective-permute-start.2) | collective-permute-done | bytes 131104 | tf_op jit(solution)/shard_map/ppermute | solution.py:272
  15.9 3.3 %collective-permute-start.4 = (bf16[4,32,1024]{2,1,0:T(8,128)(2,1)S(1)}, bf16[4,32,1024]{2,1,0:T(8,128)(2,1)S(1)}, u32[]{:S(2)}, u32[]{:S(2)}) collective-permute-start(bf16[4,32,1024]{2,1,0:T(8,128)(2,1)S(1)} %pad_maximum_fusion), channel_id=1, source_target_pairs={{14,15},{15,14},{10,11},{11,10},{6,7},{7,6},{2,3},{3,2},{0,1},{1,0... | collective-permute-start | bytes 786440 | tf_op jit(solution)/shard_map/ppermute | solution.py:276
  19.2 0.2 collective-permute-start.5
  19.4 0.9 %collective-permute-done.4.refs_4_ = bf16[4,32,1024]{2,1,0:T(8,128)(2,1)S(1)} collective-permute-done((bf16[4,32,1024]{2,1,0:T(8,128)(2,1)S(1)}, bf16[4,32,1024]{2,1,0:T(8,128)(2,1)S(1)}, u32[]{:S(2)}, u32[]{:S(2)}) %collective-permute-start.4) | collective-permute-done | bytes 262176 | tf_op jit(solution)/shard_map/ppermute | solution.py:276
  20.4 4.0 %band_inner.1 = (f32[8,1,1024]{2,1,0:T(1,128)S(1)}, bf16[4,1664,128]{2,1,0:T(8,128)(2,1)S(1)}, bf16[4,128,1024]{2,1,0:T(8,128)(2,1)S(1)}) custom-call(s32[25]{0:T(128)S(1)} %pad_add_fusion.numbers, bf16[2,32,1024]{2,1,0:T(8,128)(2,1)S(1)} %broadcast_select_fusion.1.refs_0_, bf16[2,32,1024]{2,1,0:T(8,128)(2,1)S(1)} %collective-permute-done.1.refs_1_, ...), custom_call_target="tpu_custom_call" | custom-call | tf_op jit(solution)/shard_map/band_inner/pallas_call | solution.py:176
  24.4 0.8 %collective-permute-done.5.rim = bf16[4,32,1024]{2,1,0:T(8,128)(2,1)S(1)} collective-permute-done((bf16[4,32,1024]{2,1,0:T(8,128)(2,1)S(1)}, bf16[4,32,1024]{2,1,0:T(8,128)(2,1)S(1)}, u32[]{:S(2)}, u32[]{:S(2)}) %collective-permute-start.5) | collective-permute-done | bytes 262176 | tf_op jit(solution)/shard_map/ppermute | solution.py:277
  25.1 2.6 %band_given.1 = (f32[2,2,2,1024]{3,2,1,0:T(2,128)S(1)}, bf16[4,1664,128]{2,1,0:T(8,128)(2,1)S(1)}, bf16[4,128,1024]{2,1,0:T(8,128)(2,1)S(1)}) custom-call(s32[25]{0:T(128)S(1)} %pad_add_fusion.numbers, bf16[4,32,1024]{2,1,0:T(8,128)(2,1)S(1)} %collective-permute-done.5.rim, ...), custom_call_target="tpu_custom_call", output_to_operand_aliasing={{1}: (3, {}), {2}: (4, {})} | custom-call | tf_op jit(solution)/shard_map/band_given/pallas_call | solution.py:218
  27.8 0.1 collective-permute-start.6
  27.8 2.0 %band_kept.1 = f32[2,2,2,1024]{3,2,1,0:T(2,128)S(1)} custom-call(s32[25]{0:T(128)S(1)} %pad_add_fusion.numbers, f32[8,1,1024]{2,1,0:T(1,128)S(1)} %get-tuple-element.21.done, bf16[4,1664,128]{2,1,0:T(8,128)(2,1)S(1)} %get-tuple-element.24.right, bf16[4,128,1024]{2,1,0:T(8,128)(2,1)S(1)} %get-tuple-element.25.left), custom_call_target="tpu_custom_call" | custom-call | tf_op jit(solution)/shard_map/band_kept/pallas_call | solution.py:243
  29.9 1.6 %collective-permute-start.7 = (f32[2,4,1024]{2,1,0:T(4,128)S(1)}, f32[2,4,1024]{2,1,0:T(4,128)S(1)}, u32[]{:S(2)}, u32[]{:S(2)}) collective-permute-start(f32[2,4,1024]{2,1,0:T(4,128)S(1)} %get-tuple-element.39), channel_id=1, source_target_pairs={{11,2},{7,3},{15,6},{3,7},{14,10},{2,11},{10,14},{6,15},{0,4},{12,... | collective-permute-start | bytes 98312 | tf_op jit(solution)/shard_map/ppermute | solution.py:283
  31.5 1.3 %collective-permute-start.8 = (f32[2,4,1024]{2,1,0:T(4,128)S(1)}, f32[2,4,1024]{2,1,0:T(4,128)S(1)}, u32[]{:S(2)}, u32[]{:S(2)}) collective-permute-start(f32[2,4,1024]{2,1,0:T(4,128)S(1)} %get-tuple-element.40), channel_id=1, source_target_pairs={{15,2},{7,3},{11,6},{3,7},{14,10},{6,11},{10,14},{2,15},{0,4},{8,5... | collective-permute-start | bytes 98312 | tf_op jit(solution)/shard_map/ppermute | solution.py:283
  32.8 1.8 %collective-permute-done.7 = f32[2,4,1024]{2,1,0:T(4,128)S(1)} collective-permute-done((f32[2,4,1024]{2,1,0:T(4,128)S(1)}, f32[2,4,1024]{2,1,0:T(4,128)S(1)}, u32[]{:S(2)}, u32[]{:S(2)}) %collective-permute-start.7) | collective-permute-done | bytes 32800 | tf_op jit(solution)/shard_map/ppermute | solution.py:283
  34.6 2.1 %collective-permute-done.8 = f32[2,4,1024]{2,1,0:T(4,128)S(1)} collective-permute-done((f32[2,4,1024]{2,1,0:T(4,128)S(1)}, f32[2,4,1024]{2,1,0:T(4,128)S(1)}, u32[]{:S(2)}, u32[]{:S(2)}) %collective-permute-start.8) | collective-permute-done | bytes 32800 | tf_op jit(solution)/shard_map/ppermute | solution.py:283
  36.7 0.7 %maximum_select_fusion.1 = f32[2,8,1024]{2,1,0:T(8,128)} fusion(f32[2,4,1024]{2,1,0:T(4,128)S(1)} %collective-permute-done.8, f32[2,4,1024]{2,1,0:T(4,128)S(1)} %broadcast_select_fusion.2, pred[]{:T(512)S(6)} %eq.21), kind=kLoop, calls=%fused_computation.5 | loop fusion | flops 49152 | bytes 131073 | tf_op jit(solution)/shard_map/jit(_where)/select_n | solution.py:285
  (19 shorter events, 0.3 us)
Async XLA Ops:
  0.0 8.6 %copy-start = (s32[2,4]{1,0:T(2,128)S(1)}, s32[2,4]{1,0:T(2,128)}, u32[]{:S(2)}) copy-start(s32[2,4]{1,0:T(2,128)} %param.7) | copy-start | bytes 100
  0.0 8.7 %copy-start.1 = (s32[2,4]{1,0:T(2,128)S(1)}, s32[2,4]{1,0:T(2,128)}, u32[]{:S(2)}) copy-start(s32[2,4]{1,0:T(2,128)} %param.8) | copy-start | bytes 100
  0.0 8.8 %copy-start.2 = (s32[2,4]{1,0:T(2,128)S(1)}, s32[2,4]{1,0:T(2,128)}, u32[]{:S(2)}) copy-start(s32[2,4]{1,0:T(2,128)} %param.9) | copy-start | bytes 100
  2.1 7.0 %collective-permute-start = (bf16[2,32,1024]{2,1,0:T(8,128)(2,1)S(1)}, bf16[2,32,1024]{2,1,0:T(8,128)(2,1)S(1)}, u32[]{:S(2)}, u32[]{:S(2)}) collective-permute-start(bf16[2,32,1024]{2,1,0:T(8,128)(2,1)S(1)} %get-tuple-element.30), channel_id=1, source_target_pairs={{2,11},{3,7},{6,15},{7,3},{10,14},{11,2},{14,10},{15,6},{4,0},{5,1... | collective-permute-start | bytes 393224 | tf_op jit(solution)/shard_map/ppermute | solution.py:272
  5.8 6.0 %collective-permute-start.3 = (bf16[2,32,1024]{2,1,0:T(8,128)(2,1)S(1)}, bf16[2,32,1024]{2,1,0:T(8,128)(2,1)S(1)}, u32[]{:S(2)}, u32[]{:S(2)}) collective-permute-start(bf16[2,32,1024]{2,1,0:T(8,128)(2,1)S(1)} %get-tuple-element.27), channel_id=1, source_target_pairs={{2,14},{3,6},{6,10},{7,2},{10,15},{11,7},{14,11},{15,3},{4,1},{5,9... | collective-permute-start | bytes 393224 | tf_op jit(solution)/shard_map/ppermute | solution.py:272
  6.4 9.4 %collective-permute-start.2 = (bf16[2,32,1024]{2,1,0:T(8,128)(2,1)S(1)}, bf16[2,32,1024]{2,1,0:T(8,128)(2,1)S(1)}, u32[]{:S(2)}, u32[]{:S(2)}) collective-permute-start(bf16[2,32,1024]{2,1,0:T(8,128)(2,1)S(1)} %get-tuple-element.28), channel_id=1, source_target_pairs={{2,15},{3,7},{6,11},{7,3},{10,14},{11,6},{14,10},{15,2},{4,0},{5,8... | collective-permute-start | bytes 393224 | tf_op jit(solution)/shard_map/ppermute | solution.py:272
  8.6 7.2 %collective-permute-start.1 = (bf16[2,32,1024]{2,1,0:T(8,128)(2,1)S(1)}, bf16[2,32,1024]{2,1,0:T(8,128)(2,1)S(1)}, u32[]{:S(2)}, u32[]{:S(2)}) collective-permute-start(bf16[2,32,1024]{2,1,0:T(8,128)(2,1)S(1)} %get-tuple-element.29), channel_id=1, source_target_pairs={{2,10},{3,2},{6,14},{7,6},{10,11},{11,3},{14,15},{15,7},{4,5},{5,1... | collective-permute-start | bytes 393224 | tf_op jit(solution)/shard_map/ppermute | solution.py:272
  15.9 4.4 %collective-permute-start.4 = (bf16[4,32,1024]{2,1,0:T(8,128)(2,1)S(1)}, bf16[4,32,1024]{2,1,0:T(8,128)(2,1)S(1)}, u32[]{:S(2)}, u32[]{:S(2)}) collective-permute-start(bf16[4,32,1024]{2,1,0:T(8,128)(2,1)S(1)} %pad_maximum_fusion), channel_id=1, source_target_pairs={{14,15},{15,14},{10,11},{11,10},{6,7},{7,6},{2,3},{3,2},{0,1},{1,0... | collective-permute-start | bytes 786440 | tf_op jit(solution)/shard_map/ppermute | solution.py:276
  19.2 5.9 %collective-permute-start.5 = (bf16[4,32,1024]{2,1,0:T(8,128)(2,1)S(1)}, bf16[4,32,1024]{2,1,0:T(8,128)(2,1)S(1)}, u32[]{:S(2)}, u32[]{:S(2)}) collective-permute-start(bf16[4,32,1024]{2,1,0:T(8,128)(2,1)S(1)} %pad_maximum_fusion.1), channel_id=1, source_target_pairs={{15,10},{11,6},{7,2},{3,0},{1,4},{5,8},{9,12},{13,14},{10,15},{6,1... | collective-permute-start | bytes 786440 | tf_op jit(solution)/shard_map/ppermute | solution.py:277
  27.8 2.1 %collective-permute-start.6 = (f32[2,2,2,1024]{3,2,1,0:T(2,128)S(1)}, f32[2,2,2,1024]{3,2,1,0:T(2,128)S(1)}, u32[]{:S(2)}, u32[]{:S(2)}) collective-permute-start(f32[2,2,2,1024]{3,2,1,0:T(2,128)S(1)} %get-tuple-element.26), channel_id=1, source_target_pairs={{14,15},{15,14},{10,11},{11,10},{6,7},{7,6},{2,3},{3,2},{0,1},{1,0... | collective-permute-start | bytes 98312 | tf_op jit(solution)/shard_map/ppermute | solution.py:280
  29.9 4.7 %collective-permute-start.7 = (f32[2,4,1024]{2,1,0:T(4,128)S(1)}, f32[2,4,1024]{2,1,0:T(4,128)S(1)}, u32[]{:S(2)}, u32[]{:S(2)}) collective-permute-start(f32[2,4,1024]{2,1,0:T(4,128)S(1)} %get-tuple-element.39), channel_id=1, source_target_pairs={{11,2},{7,3},{15,6},{3,7},{14,10},{2,11},{10,14},{6,15},{0,4},{12,... | collective-permute-start | bytes 98312 | tf_op jit(solution)/shard_map/ppermute | solution.py:283
  31.5 5.1 %collective-permute-start.8 = (f32[2,4,1024]{2,1,0:T(4,128)S(1)}, f32[2,4,1024]{2,1,0:T(4,128)S(1)}, u32[]{:S(2)}, u32[]{:S(2)}) collective-permute-start(f32[2,4,1024]{2,1,0:T(4,128)S(1)} %get-tuple-element.40), channel_id=1, source_target_pairs={{15,2},{7,3},{11,6},{3,7},{14,10},{6,11},{10,14},{2,15},{0,4},{8,5... | collective-permute-start | bytes 98312 | tf_op jit(solution)/shard_map/ppermute | solution.py:283

commit v5 on v4

--- a/solution.py
+++ b/solution.py
@@ -148,12 +148,12 @@
     return [jnp.full((channels, BX), w).astype(jnp.bfloat16) for w in (0.75 - heavy, heavy)]
 
 
-def band_inner(numbers, base, rim):
+def band_inner(numbers, kept, base, rim):
     _, channels, columns = base[0].shape
     depth = 4 * channels
 
     def body(numbers, *refs):
-        base, (rim, result, right, outer_left, left) = refs[:VIEWS], refs[VIEWS:]
+        kept, base, (rim, result, right, outer_left, left) = refs[0], refs[1 : VIEWS + 1], refs[VIEWS + 1 :]
         at = Place(numbers[3 * PAIRS])
         beside = Place(at.place + 1 - 2 * at.core)
         inner, outer = shares_of(1 - at.core, channels), shares_of(at.core, channels)
@@ -164,6 +164,8 @@
             for n in range(columns // BX):
                 span = slice(n * BX, (n + 1) * BX)
                 pair = [base[m][0, :, span], base[m][1, :, span]]
+                if m == 0:
+                    pair = [jnp.where(at.slot // 2 == at.core, kept[r, :, span], pair[r]) for r in range(2)]
                 third = rim[there, :, span]
                 right[m, PAD + n * BX : PAD + (n + 1) * BX, :] = jnp.concatenate([third] + pair + [nothing], 0).T
                 mixed = [r * w for r, w in zip(pair, inner)]
@@ -180,12 +182,12 @@
             jax.ShapeDtypeStruct((VIEWS, PAD + columns, depth), jnp.bfloat16),
             jax.ShapeDtypeStruct((VIEWS, depth, columns), jnp.bfloat16),
         ],
-        in_specs=[pl.BlockSpec(memory_space=pltpu.SMEM)] + [vmem] * (VIEWS + 1),
+        in_specs=[pl.BlockSpec(memory_space=pltpu.SMEM)] + [vmem] * (VIEWS + 2),
         out_specs=[vmem] * 3,
         scratch_shapes=[pltpu.VMEM((VIEWS, depth, columns), jnp.bfloat16)],
         compiler_params=pltpu.CompilerParams(vmem_limit_bytes=48 << 20),
         name="band_inner",
-    )(numbers, *base, rim)
+    )(numbers, kept, *base, rim)
 
 
 def both_rows(core, first, second, group, out):
@@ -260,7 +262,7 @@
     view, spot = index // per_view, index % per_view
     unit, core = spot // 2, spot % 2
     slot = jnp.where(unit % 2 == 1, (view + 1) % VIEWS, VIEWS - 1 - view)
-    first = (slot % 2) * 2 + slot // 2
+    first = ((slot % 2) * 2 + slot // 2)
     place = 8 * unit + 2 * slot + core
     numbers = jnp.concatenate(
         [left_views.reshape(-1), right_step.reshape(-1), offset_tile.reshape(-1), place.astype(jnp.int32).reshape(1)]
@@ -270,12 +272,13 @@
     stays = slot // 2 == core
     pieces = [lax.dynamic_slice_in_dim(masked, 2 * (first ^ m), 2, 0) for m in range(VIEWS)]
     base = [lax.ppermute(pieces[m], "strip", share[m]) for m in range(VIEWS)]
-    base[0] = jnp.where(stays, pieces[0], base[0])
     numbers, base = lax.optimization_barrier((numbers, base))
-    rows = [jnp.concatenate([lax.dynamic_slice_in_dim(g, r, 1, 0) for g in base], 0) for r in (1 - core, core)]
+    whole = list(base)
+    whole[0] = jnp.where(stays, pieces[0], base[0])
+    rows = [jnp.concatenate([lax.dynamic_slice_in_dim(g, r, 1, 0) for g in whole], 0) for r in (1 - core, core)]
     beside = lax.ppermute(rows[0], "strip", siblings)
     beyond = lax.ppermute(rows[1], "strip", neighbours)
-    done, right, left = band_inner(numbers, base, beside)
+    done, right, left = band_inner(numbers, pieces[0], base, beside)
     given, right, left = band_given(numbers, beyond, done, right, left, strips)
     taken = lax.ppermute(given, "strip", siblings)
     kept = band_kept(numbers, done, right, left)

time: 37.5 us -> 36.3 us (0.968)
  starting transfers between devices: 13 us -> 8.47 us
  waiting for transfers between devices: 12.4 us -> 15.7 us
    ppermute x4, waiting for transfers between devices: 6.84 us -> 10.6 us  [per_device(): base = [lax.ppermute(pieces[m], 'strip', share[m]) for m in range(VIEWS)]]
    ppermute x1, starting transfers between devices: 3.28 us -> 0.07 us  [per_device(): beside = lax.ppermute(rows[0], 'strip', siblings)]
    ppermute x4, starting transfers between devices: 6.58 us -> 5.75 us  [per_device(): base = [lax.ppermute(pieces[m], 'strip', share[m]) for m in range(VIEWS)]]
    ppermute x2, starting transfers between devices: 2.9 us -> 2.13 us  [per_device(): back = [lax.ppermute(sent[e], 'strip', home[e]) for e in range(2)]]
    ppermute x2, waiting for transfers between devices: 3.84 us -> 3.18 us  [per_device(): back = [lax.ppermute(sent[e], 'strip', home[e]) for e in range(2)]]
    ppermute x1, waiting for transfers between devices: 0.94 us -> 1.4 us  [per_device(): beside = lax.ppermute(rows[0], 'strip', siblings)]
  transfers between devices with their start and end apart: 9 -> 9, of which waited for: 7 -> 7; matrix products, arithmetic and copies ran while one was open for 1% -> 1% of each run, Pallas kernels for 16% -> 17%
where the time goes in v5:
time: 36.3 us; the launch traced here: 36.2 us
  waiting for transfers between devices  15.7 us (43%)
  Pallas kernels  8.64 us (24%)
  starting transfers between devices  8.47 us (23%)
  other arithmetic  2.05 us (6%)
  between operations  0.93 us (3%)
  local copies, waits for them, and re-layouts  0.37 us (1%)
    ppermute x4, waiting for transfers between devices, per_device(): base = [lax.ppermute(pieces[m], 'strip', share[m]) for m in range(VIEWS)]  10.6 us
    ppermute x4, starting transfers between devices, per_device(): base = [lax.ppermute(pieces[m], 'strip', share[m]) for m in range(VIEWS)]  5.75 us
    pallas_call x1, Pallas kernels, band_inner(): pl.pallas_call(body, out_shape=[jax.ShapeDtypeStruct((PAIRS, 1, columns),...  3.98 us
    ppermute x2, waiting for transfers between devices, per_device(): back = [lax.ppermute(sent[e], 'strip', home[e]) for e in range(2)]  3.18 us
    pallas_call x1, Pallas kernels, band_given(): pl.pallas_call(body, out_shape=[jax.ShapeDtypeStruct((2, ROUNDS, 2, colum...  2.65 us
    ppermute x2, starting transfers between devices, per_device(): back = [lax.ppermute(sent[e], 'strip', home[e]) for e in range(2)]  2.13 us
    pallas_call x1, Pallas kernels, band_kept(): pl.pallas_call(body, out_shape=jax.ShapeDtypeStruct((2, ROUNDS, 2, column...  2.01 us
    ppermute x1, waiting for transfers between devices, per_device(): beside = lax.ppermute(rows[0], 'strip', siblings)  1.4 us
  transfers between devices with their start and end apart: 9, of which 7 were waited for; matrix products, arithmetic and copies ran while one was open for 1% of the time, Pallas kernels for 17%

profile of v5, /device:TPU:1, one launch (start us, length us, event | category | flops | bytes accessed | tf_op | source)
XLA Modules:
  0.0 36.2 jit_solution(17156740440936202209)
XLA Ops:
  0.8 1.1 %broadcast_select_fusion = bf16[8,32,1024]{2,1,0:T(8,128)(2,1)S(1)} fusion(bf16[8,32,1024]{2,1,0:T(8,128)(2,1)} %param.5, pred[8]{0:T(512)(128)(4,1)S(1)} %iota_compare_fusion), kind=kLoop, calls=%fused_computation | loop fusion | flops 262144 | bytes 1048584 | tf_op jit(solution)/shard_map/jit(_where)/select_n | solution.py:271
  2.1 4.2 %collective-permute-start.3 = (bf16[2,32,1024]{2,1,0:T(8,128)(2,1)S(1)}, bf16[2,32,1024]{2,1,0:T(8,128)(2,1)S(1)}, u32[]{:S(2)}, u32[]{:S(2)}) collective-permute-start(bf16[2,32,1024]{2,1,0:T(8,128)(2,1)S(1)} %get-tuple-element.27), channel_id=1, source_target_pairs={{2,14},{3,6},{6,10},{7,2},{10,15},{11,7},{14,11},{15,3},{4,1},{5,9... | collective-permute-start | bytes 393224 | tf_op jit(solution)/shard_map/ppermute | solution.py:274
  6.3 0.6 %collective-permute-start.2 = (bf16[2,32,1024]{2,1,0:T(8,128)(2,1)S(1)}, bf16[2,32,1024]{2,1,0:T(8,128)(2,1)S(1)}, u32[]{:S(2)}, u32[]{:S(2)}) collective-permute-start(bf16[2,32,1024]{2,1,0:T(8,128)(2,1)S(1)} %get-tuple-element.28), channel_id=1, source_target_pairs={{2,15},{3,7},{6,11},{7,3},{10,14},{11,6},{14,10},{15,2},{4,0},{5,8... | collective-permute-start | bytes 393224 | tf_op jit(solution)/shard_map/ppermute | solution.py:274
  6.9 0.4 %collective-permute-start.1 = (bf16[2,32,1024]{2,1,0:T(8,128)(2,1)S(1)}, bf16[2,32,1024]{2,1,0:T(8,128)(2,1)S(1)}, u32[]{:S(2)}, u32[]{:S(2)}) collective-permute-start(bf16[2,32,1024]{2,1,0:T(8,128)(2,1)S(1)} %get-tuple-element.29), channel_id=1, source_target_pairs={{2,10},{3,2},{6,14},{7,6},{10,11},{11,3},{14,15},{15,7},{4,5},{5,1... | collective-permute-start | bytes 393224 | tf_op jit(solution)/shard_map/ppermute | solution.py:274
  7.3 0.5 %collective-permute-start = (bf16[2,32,1024]{2,1,0:T(8,128)(2,1)S(1)}, bf16[2,32,1024]{2,1,0:T(8,128)(2,1)S(1)}, u32[]{:S(2)}, u32[]{:S(2)}) collective-permute-start(bf16[2,32,1024]{2,1,0:T(8,128)(2,1)S(1)} %get-tuple-element.30.refs_0_), channel_id=1, source_target_pairs={{2,11},{3,7},{6,15},{7,3},{10,14},{11,2},{14,10},{15,6},{4,0},{5,1... | collective-permute-start | bytes 393224 | tf_op jit(solution)/shard_map/ppermute | solution.py:274
  7.8 0.1 reshape.19
  7.9 0.1 reshape.20
  8.0 0.1 reshape.21
  8.1 0.1 pad_add_fusion.numbers
  8.1 1.5 %collective-permute-done.3.refs_4_ = bf16[2,32,1024]{2,1,0:T(8,128)(2,1)S(1)} collective-permute-done((bf16[2,32,1024]{2,1,0:T(8,128)(2,1)S(1)}, bf16[2,32,1024]{2,1,0:T(8,128)(2,1)S(1)}, u32[]{:S(2)}, u32[]{:S(2)}) %collective-permute-start.3) | collective-permute-done | bytes 131104 | tf_op jit(solution)/shard_map/ppermute | solution.py:274
  9.6 4.3 %collective-permute-done.2.refs_3_ = bf16[2,32,1024]{2,1,0:T(8,128)(2,1)S(1)} collective-permute-done((bf16[2,32,1024]{2,1,0:T(8,128)(2,1)S(1)}, bf16[2,32,1024]{2,1,0:T(8,128)(2,1)S(1)}, u32[]{:S(2)}, u32[]{:S(2)}) %collective-permute-start.2) | collective-permute-done | bytes 131104 | tf_op jit(solution)/shard_map/ppermute | solution.py:274
  14.0 4.8 %collective-permute-done.refs_1_ = bf16[2,32,1024]{2,1,0:T(8,128)(2,1)S(1)} collective-permute-done((bf16[2,32,1024]{2,1,0:T(8,128)(2,1)S(1)}, bf16[2,32,1024]{2,1,0:T(8,128)(2,1)S(1)}, u32[]{:S(2)}, u32[]{:S(2)}) %collective-permute-start) | collective-permute-done | bytes 131104 | tf_op jit(solution)/shard_map/ppermute | solution.py:274
  18.9 0.1 collective-permute-start.4
  19.1 1.4 %collective-permute-done.4.refs_5_ = bf16[4,32,1024]{2,1,0:T(8,128)(2,1)S(1)} collective-permute-done((bf16[4,32,1024]{2,1,0:T(8,128)(2,1)S(1)}, bf16[4,32,1024]{2,1,0:T(8,128)(2,1)S(1)}, u32[]{:S(2)}, u32[]{:S(2)}) %collective-permute-start.4) | collective-permute-done | bytes 262176 | tf_op jit(solution)/shard_map/ppermute | solution.py:279
  20.5 4.0 %band_inner.1 = (f32[8,1,1024]{2,1,0:T(1,128)S(1)}, bf16[4,1664,128]{2,1,0:T(8,128)(2,1)S(1)}, bf16[4,128,1024]{2,1,0:T(8,128)(2,1)S(1)}) custom-call(s32[25]{0:T(128)S(1)} %pad_add_fusion.numbers, bf16[2,32,1024]{2,1,0:T(8,128)(2,1)S(1)} %get-tuple-element.30.refs_0_, bf16[2,32,1024]{2,1,0:T(8,128)(2,1)S(1)} %collective-permute-done.refs_1_, ...), custom_call_target="tpu_custom_call" | custom-call | tf_op jit(solution)/shard_map/band_inner/pallas_call | solution.py:178
  24.5 0.5 %collective-permute-done.5.rim = bf16[4,32,1024]{2,1,0:T(8,128)(2,1)S(1)} collective-permute-done((bf16[4,32,1024]{2,1,0:T(8,128)(2,1)S(1)}, bf16[4,32,1024]{2,1,0:T(8,128)(2,1)S(1)}, u32[]{:S(2)}, u32[]{:S(2)}) %collective-permute-start.5) | collective-permute-done | bytes 262176 | tf_op jit(solution)/shard_map/ppermute | solution.py:280
  25.0 2.7 %band_given.1 = (f32[2,2,2,1024]{3,2,1,0:T(2,128)S(1)}, bf16[4,1664,128]{2,1,0:T(8,128)(2,1)S(1)}, bf16[4,128,1024]{2,1,0:T(8,128)(2,1)S(1)}) custom-call(s32[25]{0:T(128)S(1)} %pad_add_fusion.numbers, bf16[4,32,1024]{2,1,0:T(8,128)(2,1)S(1)} %collective-permute-done.5.rim, ...), custom_call_target="tpu_custom_call", output_to_operand_aliasing={{1}: (3, {}), {2}: (4, {})} | custom-call | tf_op jit(solution)/shard_map/band_given/pallas_call | solution.py:220
  27.7 0.4 %collective-permute-start.6 = (f32[2,2,2,1024]{3,2,1,0:T(2,128)S(1)}, f32[2,2,2,1024]{3,2,1,0:T(2,128)S(1)}, u32[]{:S(2)}, u32[]{:S(2)}) collective-permute-start(f32[2,2,2,1024]{3,2,1,0:T(2,128)S(1)} %get-tuple-element.26), channel_id=1, source_target_pairs={{14,15},{15,14},{10,11},{11,10},{6,7},{7,6},{2,3},{3,2},{0,1},{1,0... | collective-permute-start | bytes 98312 | tf_op jit(solution)/shard_map/ppermute | solution.py:283
  28.1 2.0 %band_kept.1 = f32[2,2,2,1024]{3,2,1,0:T(2,128)S(1)} custom-call(s32[25]{0:T(128)S(1)} %pad_add_fusion.numbers, f32[8,1,1024]{2,1,0:T(1,128)S(1)} %get-tuple-element.21.done, bf16[4,1664,128]{2,1,0:T(8,128)(2,1)S(1)} %get-tuple-element.24.right, bf16[4,128,1024]{2,1,0:T(8,128)(2,1)S(1)} %get-tuple-element.25.left), custom_call_target="tpu_custom_call" | custom-call | tf_op jit(solution)/shard_map/band_kept/pallas_call | solution.py:245
  30.2 0.2 collective-permute-start.7
  30.4 2.0 %collective-permute-start.8 = (f32[2,4,1024]{2,1,0:T(4,128)S(1)}, f32[2,4,1024]{2,1,0:T(4,128)S(1)}, u32[]{:S(2)}, u32[]{:S(2)}) collective-permute-start(f32[2,4,1024]{2,1,0:T(4,128)S(1)} %get-tuple-element.40), channel_id=1, source_target_pairs={{15,2},{7,3},{11,6},{3,7},{14,10},{6,11},{10,14},{2,15},{0,4},{8,5... | collective-permute-start | bytes 98312 | tf_op jit(solution)/shard_map/ppermute | solution.py:286
  32.3 2.2 %collective-permute-done.7 = f32[2,4,1024]{2,1,0:T(4,128)S(1)} collective-permute-done((f32[2,4,1024]{2,1,0:T(4,128)S(1)}, f32[2,4,1024]{2,1,0:T(4,128)S(1)}, u32[]{:S(2)}, u32[]{:S(2)}) %collective-permute-start.7) | collective-permute-done | bytes 32800 | tf_op jit(solution)/shard_map/ppermute | solution.py:286
  34.5 1.0 %collective-permute-done.8 = f32[2,4,1024]{2,1,0:T(4,128)S(1)} collective-permute-done((f32[2,4,1024]{2,1,0:T(4,128)S(1)}, f32[2,4,1024]{2,1,0:T(4,128)S(1)}, u32[]{:S(2)}, u32[]{:S(2)}) %collective-permute-start.8) | collective-permute-done | bytes 32800 | tf_op jit(solution)/shard_map/ppermute | solution.py:286
  35.5 0.7 %maximum_select_fusion.1 = f32[2,8,1024]{2,1,0:T(8,128)} fusion(f32[2,4,1024]{2,1,0:T(4,128)S(1)} %collective-permute-done.8, f32[2,4,1024]{2,1,0:T(4,128)S(1)} %broadcast_select_fusion.2, pred[]{:T(512)S(6)} %eq.21), kind=kLoop, calls=%fused_computation.5 | loop fusion | flops 49152 | bytes 131073 | tf_op jit(solution)/shard_map/jit(_where)/select_n | solution.py:288
  (19 shorter events, 0.4 us)
Async XLA Ops:
  0.0 7.8 %copy-start = (s32[2,4]{1,0:T(2,128)S(1)}, s32[2,4]{1,0:T(2,128)}, u32[]{:S(2)}) copy-start(s32[2,4]{1,0:T(2,128)} %param.7) | copy-start | bytes 100
  0.0 7.9 %copy-start.1 = (s32[2,4]{1,0:T(2,128)S(1)}, s32[2,4]{1,0:T(2,128)}, u32[]{:S(2)}) copy-start(s32[2,4]{1,0:T(2,128)} %param.8) | copy-start | bytes 100
  0.0 8.0 %copy-start.2 = (s32[2,4]{1,0:T(2,128)S(1)}, s32[2,4]{1,0:T(2,128)}, u32[]{:S(2)}) copy-start(s32[2,4]{1,0:T(2,128)} %param.9) | copy-start | bytes 100
  2.1 7.6 %collective-permute-start.3 = (bf16[2,32,1024]{2,1,0:T(8,128)(2,1)S(1)}, bf16[2,32,1024]{2,1,0:T(8,128)(2,1)S(1)}, u32[]{:S(2)}, u32[]{:S(2)}) collective-permute-start(bf16[2,32,1024]{2,1,0:T(8,128)(2,1)S(1)} %get-tuple-element.27), channel_id=1, source_target_pairs={{2,14},{3,6},{6,10},{7,2},{10,15},{11,7},{14,11},{15,3},{4,1},{5,9... | collective-permute-start | bytes 393224 | tf_op jit(solution)/shard_map/ppermute | solution.py:274
  6.3 7.7 %collective-permute-start.2 = (bf16[2,32,1024]{2,1,0:T(8,128)(2,1)S(1)}, bf16[2,32,1024]{2,1,0:T(8,128)(2,1)S(1)}, u32[]{:S(2)}, u32[]{:S(2)}) collective-permute-start(bf16[2,32,1024]{2,1,0:T(8,128)(2,1)S(1)} %get-tuple-element.28), channel_id=1, source_target_pairs={{2,15},{3,7},{6,11},{7,3},{10,14},{11,6},{14,10},{15,2},{4,0},{5,8... | collective-permute-start | bytes 393224 | tf_op jit(solution)/shard_map/ppermute | solution.py:274
  6.9 7.1 %collective-permute-start.1 = (bf16[2,32,1024]{2,1,0:T(8,128)(2,1)S(1)}, bf16[2,32,1024]{2,1,0:T(8,128)(2,1)S(1)}, u32[]{:S(2)}, u32[]{:S(2)}) collective-permute-start(bf16[2,32,1024]{2,1,0:T(8,128)(2,1)S(1)} %get-tuple-element.29), channel_id=1, source_target_pairs={{2,10},{3,2},{6,14},{7,6},{10,11},{11,3},{14,15},{15,7},{4,5},{5,1... | collective-permute-start | bytes 393224 | tf_op jit(solution)/shard_map/ppermute | solution.py:274
  7.3 11.5 %collective-permute-start = (bf16[2,32,1024]{2,1,0:T(8,128)(2,1)S(1)}, bf16[2,32,1024]{2,1,0:T(8,128)(2,1)S(1)}, u32[]{:S(2)}, u32[]{:S(2)}) collective-permute-start(bf16[2,32,1024]{2,1,0:T(8,128)(2,1)S(1)} %get-tuple-element.30.refs_0_), channel_id=1, source_target_pairs={{2,11},{3,7},{6,15},{7,3},{10,14},{11,2},{14,10},{15,6},{4,0},{5,1... | collective-permute-start | bytes 393224 | tf_op jit(solution)/shard_map/ppermute | solution.py:274
  18.9 1.6 %collective-permute-start.4 = (bf16[4,32,1024]{2,1,0:T(8,128)(2,1)S(1)}, bf16[4,32,1024]{2,1,0:T(8,128)(2,1)S(1)}, u32[]{:S(2)}, u32[]{:S(2)}) collective-permute-start(bf16[4,32,1024]{2,1,0:T(8,128)(2,1)S(1)} %pad_maximum_fusion), channel_id=1, source_target_pairs={{14,15},{15,14},{10,11},{11,10},{6,7},{7,6},{2,3},{3,2},{0,1},{1,0... | collective-permute-start | bytes 786440 | tf_op jit(solution)/shard_map/ppermute | solution.py:279
  19.0 6.0 %collective-permute-start.5 = (bf16[4,32,1024]{2,1,0:T(8,128)(2,1)S(1)}, bf16[4,32,1024]{2,1,0:T(8,128)(2,1)S(1)}, u32[]{:S(2)}, u32[]{:S(2)}) collective-permute-start(bf16[4,32,1024]{2,1,0:T(8,128)(2,1)S(1)} %pad_maximum_fusion.1), channel_id=1, source_target_pairs={{15,10},{11,6},{7,2},{3,0},{1,4},{5,8},{9,12},{13,14},{10,15},{6,1... | collective-permute-start | bytes 786440 | tf_op jit(solution)/shard_map/ppermute | solution.py:280
  27.7 2.5 %collective-permute-start.6 = (f32[2,2,2,1024]{3,2,1,0:T(2,128)S(1)}, f32[2,2,2,1024]{3,2,1,0:T(2,128)S(1)}, u32[]{:S(2)}, u32[]{:S(2)}) collective-permute-start(f32[2,2,2,1024]{3,2,1,0:T(2,128)S(1)} %get-tuple-element.26), channel_id=1, source_target_pairs={{14,15},{15,14},{10,11},{11,10},{6,7},{7,6},{2,3},{3,2},{0,1},{1,0... | collective-permute-start | bytes 98312 | tf_op jit(solution)/shard_map/ppermute | solution.py:283
  30.2 4.3 %collective-permute-start.7 = (f32[2,4,1024]{2,1,0:T(4,128)S(1)}, f32[2,4,1024]{2,1,0:T(4,128)S(1)}, u32[]{:S(2)}, u32[]{:S(2)}) collective-permute-start(f32[2,4,1024]{2,1,0:T(4,128)S(1)} %get-tuple-element.39), channel_id=1, source_target_pairs={{11,2},{7,3},{15,6},{3,7},{14,10},{2,11},{10,14},{6,15},{0,4},{12,... | collective-permute-start | bytes 98312 | tf_op jit(solution)/shard_map/ppermute | solution.py:286
  30.4 5.2 %collective-permute-start.8 = (f32[2,4,1024]{2,1,0:T(4,128)S(1)}, f32[2,4,1024]{2,1,0:T(4,128)S(1)}, u32[]{:S(2)}, u32[]{:S(2)}) collective-permute-start(f32[2,4,1024]{2,1,0:T(4,128)S(1)} %get-tuple-element.40), channel_id=1, source_target_pairs={{15,2},{7,3},{11,6},{3,7},{14,10},{6,11},{10,14},{2,15},{0,4},{8,5... | collective-permute-start | bytes 98312 | tf_op jit(solution)/shard_map/ppermute | solution.py:286

commit v6 on v5

--- a/solution.py
+++ b/solution.py
@@ -71,8 +71,8 @@
     groups = BX // 8
 
     def part(span, a):
-        first = (span + half) * BX + 8 * a
-        return scores[first : first + 8, half * BX : (half + 1) * BX]
+        first = (span + half) % 2 * BX + 8 * a
+        return scores[(span + half) // 2][first : first + 8, half * BX : (half + 1) * BX]
 
     near = [jnp.where(x_less_b < 8 * a, part(0, a), part(2, a)) for a in range(groups)]
     far = [part(1, a) for a in range(groups)]
@@ -99,22 +99,22 @@
 class Place:
     def __init__(self, place):
         self.place = place
-        self.unit, self.slot, self.core = place // 8, place % 8 // 2, place % 2
+        self.unit, self.slot, self.core = place >> 3, (place >> 1) & 3, place & 1
 
     def slot_of(self, view):
-        return jnp.where(self.unit % 2 == 1, (view + 1) % VIEWS, VIEWS - 1 - view)
+        return jnp.where((self.unit & 1) == 1, (view + 1) & (VIEWS - 1), VIEWS - 1 - view)
 
     def view_at(self, slot):
-        return jnp.where(self.unit % 2 == 1, (slot + VIEWS - 1) % VIEWS, VIEWS - 1 - slot)
+        return jnp.where((self.unit & 1) == 1, (slot + VIEWS - 1) & (VIEWS - 1), VIEWS - 1 - slot)
 
     def view_of(self, buffer):
-        return self.view_at(swap_bits((self.place % 4) ^ buffer))
+        return self.view_at(swap_bits((self.place & 3) ^ buffer))
 
     def buffer_of(self, view):
-        return (self.place % 4) ^ swap_bits(self.slot_of(view))
+        return (self.place & 3) ^ swap_bits(self.slot_of(view))
 
     def view_home(self, group, e):
-        return self.view_at(2 * (self.core ^ group) + (e ^ 1 ^ (self.slot % 2)))
+        return self.view_at(2 * (self.core ^ group) + (e ^ 1 ^ (self.slot & 1)))
 
 
 def correlate(numbers, at, right, left, result, groups):
@@ -122,20 +122,23 @@
     x_less_b = lax.broadcasted_iota(jnp.int32, (8, BX), 1) - lax.broadcasted_iota(jnp.int32, (8, BX), 0)
 
     def one_pair(i, carry):
-        q, e, group = i % 2, i // 2 % 2, i // 4
+        q, e, group = i & 1, (i >> 1) & 1, i >> 2
         j = VIEWS * q + at.view_home(group, e)
         left_view = numbers[j]
-        right_view = (left_view + numbers[PAIRS + j]) % VIEWS
+        right_view = (left_view + numbers[PAIRS + j]) & (VIEWS - 1)
         tile = numbers[2 * PAIRS + j]
         a, b = at.buffer_of(left_view), at.buffer_of(right_view)
         shift = (tile * BX).astype(jnp.float32)
         for n in range(0, columns // BX, 2):
             start = pl.multiple_of((TILES - 1 + n - tile) * BX, BX)
-            scores = jnp.dot(
-                right[b, pl.ds(start, 2 * BX + LEVELS), :],
-                left[a, :, n * BX : (n + 2) * BX],
-                preferred_element_type=jnp.float32,
-            )
+            scores = [
+                jnp.dot(
+                    right[b, pl.ds(start + i * 2 * BX, 2 * BX), :],
+                    left[a, :, n * BX : (n + 2) * BX],
+                    preferred_element_type=jnp.float32,
+                )
+                for i in range(2)
+            ]
             for k in range(2):
                 result[i, :, (n + k) * BX : (n + k + 1) * BX] = regress(scores, k, x_less_b) + shift
         return carry
@@ -165,7 +168,7 @@
                 span = slice(n * BX, (n + 1) * BX)
                 pair = [base[m][0, :, span], base[m][1, :, span]]
                 if m == 0:
-                    pair = [jnp.where(at.slot // 2 == at.core, kept[r, :, span], pair[r]) for r in range(2)]
+                    pair = [jnp.where((at.slot >> 1) == at.core, kept[r, :, span], pair[r]) for r in range(2)]
                 third = rim[there, :, span]
                 right[m, PAD + n * BX : PAD + (n + 1) * BX, :] = jnp.concatenate([third] + pair + [nothing], 0).T
                 mixed = [r * w for r, w in zip(pair, inner)]
@@ -203,7 +206,8 @@
 
     def body(numbers, rim, done, right_in, left_in, given, right, left, result):
         at = Place(numbers[3 * PAIRS])
-        beyond = Place((at.place - 1 + 2 * at.core + places) % places)
+        neighbour = at.place - 1 + 2 * at.core
+        beyond = Place(jnp.where(neighbour < 0, places - 1, jnp.where(neighbour == places, 0, neighbour)))
         edge = at.place == jnp.where(at.core == 0, 0, places - 1)
         share = jnp.full((channels, BX), jnp.where(edge, 0.0, 0.25)).astype(jnp.bfloat16)
         for m in range(VIEWS):

time: 36.3 us -> 36.3 us (level)
  transfers between devices with their start and end apart: 9 -> 9, of which waited for: 7 -> 7; matrix products, arithmetic and copies ran while one was open for 1% -> 1% of each run, Pallas kernels for 17% -> 16%
where the time goes in v6:
time: 36.3 us; the launch traced here: 36.1 us
  waiting for transfers between devices  15.8 us (44%)
  starting transfers between devices  8.5 us (23%)
  Pallas kernels  8.42 us (23%)
  other arithmetic  2.05 us (6%)
  between operations  0.93 us (3%)
  local copies, waits for them, and re-layouts  0.37 us (1%)
    ppermute x4, waiting for transfers between devices, per_device(): base = [lax.ppermute(pieces[m], 'strip', share[m]) for m in range(VIEWS)]  10.6 us
    ppermute x4, starting transfers between devices, per_device(): base = [lax.ppermute(pieces[m], 'strip', share[m]) for m in range(VIEWS)]  5.75 us
    pallas_call x1, Pallas kernels, band_inner(): pl.pallas_call(body, out_shape=[jax.ShapeDtypeStruct((PAIRS, 1, columns),...  3.86 us
    ppermute x2, waiting for transfers between devices, per_device(): back = [lax.ppermute(sent[e], 'strip', home[e]) for e in range(2)]  3.16 us
    pallas_call x1, Pallas kernels, band_given(): pl.pallas_call(body, out_shape=[jax.ShapeDtypeStruct((2, ROUNDS, 2, colum...  2.63 us
    ppermute x2, starting transfers between devices, per_device(): back = [lax.ppermute(sent[e], 'strip', home[e]) for e in range(2)]  2.13 us
    pallas_call x1, Pallas kernels, band_kept(): pl.pallas_call(body, out_shape=jax.ShapeDtypeStruct((2, ROUNDS, 2, column...  1.94 us
    ppermute x1, waiting for transfers between devices, per_device(): beside = lax.ppermute(rows[0], 'strip', siblings)  1.4 us
  transfers between devices with their start and end apart: 9, of which 7 were waited for; matrix products, arithmetic and copies ran while one was open for 1% of the time, Pallas kernels for 16%

profile of v6, /device:TPU:1, one launch (start us, length us, event | category | flops | bytes accessed | tf_op | source)
XLA Modules:
  0.0 36.1 jit_solution(3227938349179682782)
XLA Ops:
  0.8 1.1 %broadcast_select_fusion = bf16[8,32,1024]{2,1,0:T(8,128)(2,1)S(1)} fusion(bf16[8,32,1024]{2,1,0:T(8,128)(2,1)} %param.5, pred[8]{0:T(512)(128)(4,1)S(1)} %iota_compare_fusion), kind=kLoop, calls=%fused_computation | loop fusion | flops 262144 | bytes 1048584 | tf_op jit(solution)/shard_map/jit(_where)/select_n | solution.py:275
  2.1 4.2 %collective-permute-start.3 = (bf16[2,32,1024]{2,1,0:T(8,128)(2,1)S(1)}, bf16[2,32,1024]{2,1,0:T(8,128)(2,1)S(1)}, u32[]{:S(2)}, u32[]{:S(2)}) collective-permute-start(bf16[2,32,1024]{2,1,0:T(8,128)(2,1)S(1)} %get-tuple-element.27), channel_id=1, source_target_pairs={{2,14},{3,6},{6,10},{7,2},{10,15},{11,7},{14,11},{15,3},{4,1},{5,9... | collective-permute-start | bytes 393224 | tf_op jit(solution)/shard_map/ppermute | solution.py:278
  6.3 0.6 %collective-permute-start.2 = (bf16[2,32,1024]{2,1,0:T(8,128)(2,1)S(1)}, bf16[2,32,1024]{2,1,0:T(8,128)(2,1)S(1)}, u32[]{:S(2)}, u32[]{:S(2)}) collective-permute-start(bf16[2,32,1024]{2,1,0:T(8,128)(2,1)S(1)} %get-tuple-element.28), channel_id=1, source_target_pairs={{2,15},{3,7},{6,11},{7,3},{10,14},{11,6},{14,10},{15,2},{4,0},{5,8... | collective-permute-start | bytes 393224 | tf_op jit(solution)/shard_map/ppermute | solution.py:278
  6.9 0.4 %collective-permute-start.1 = (bf16[2,32,1024]{2,1,0:T(8,128)(2,1)S(1)}, bf16[2,32,1024]{2,1,0:T(8,128)(2,1)S(1)}, u32[]{:S(2)}, u32[]{:S(2)}) collective-permute-start(bf16[2,32,1024]{2,1,0:T(8,128)(2,1)S(1)} %get-tuple-element.29), channel_id=1, source_target_pairs={{2,10},{3,2},{6,14},{7,6},{10,11},{11,3},{14,15},{15,7},{4,5},{5,1... | collective-permute-start | bytes 393224 | tf_op jit(solution)/shard_map/ppermute | solution.py:278
  7.3 0.5 %collective-permute-start = (bf16[2,32,1024]{2,1,0:T(8,128)(2,1)S(1)}, bf16[2,32,1024]{2,1,0:T(8,128)(2,1)S(1)}, u32[]{:S(2)}, u32[]{:S(2)}) collective-permute-start(bf16[2,32,1024]{2,1,0:T(8,128)(2,1)S(1)} %get-tuple-element.30.refs_0_), channel_id=1, source_target_pairs={{2,11},{3,7},{6,15},{7,3},{10,14},{11,2},{14,10},{15,6},{4,0},{5,1... | collective-permute-start | bytes 393224 | tf_op jit(solution)/shard_map/ppermute | solution.py:278
  7.8 0.1 reshape.19
  7.9 0.1 reshape.20
  8.0 0.1 reshape.21
  8.1 0.1 pad_add_fusion.numbers
  8.1 1.5 %collective-permute-done.3.refs_4_ = bf16[2,32,1024]{2,1,0:T(8,128)(2,1)S(1)} collective-permute-done((bf16[2,32,1024]{2,1,0:T(8,128)(2,1)S(1)}, bf16[2,32,1024]{2,1,0:T(8,128)(2,1)S(1)}, u32[]{:S(2)}, u32[]{:S(2)}) %collective-permute-start.3) | collective-permute-done | bytes 131104 | tf_op jit(solution)/shard_map/ppermute | solution.py:278
  9.6 4.3 %collective-permute-done.2.refs_3_ = bf16[2,32,1024]{2,1,0:T(8,128)(2,1)S(1)} collective-permute-done((bf16[2,32,1024]{2,1,0:T(8,128)(2,1)S(1)}, bf16[2,32,1024]{2,1,0:T(8,128)(2,1)S(1)}, u32[]{:S(2)}, u32[]{:S(2)}) %collective-permute-start.2) | collective-permute-done | bytes 131104 | tf_op jit(solution)/shard_map/ppermute | solution.py:278
  14.0 4.8 %collective-permute-done.refs_1_ = bf16[2,32,1024]{2,1,0:T(8,128)(2,1)S(1)} collective-permute-done((bf16[2,32,1024]{2,1,0:T(8,128)(2,1)S(1)}, bf16[2,32,1024]{2,1,0:T(8,128)(2,1)S(1)}, u32[]{:S(2)}, u32[]{:S(2)}) %collective-permute-start) | collective-permute-done | bytes 131104 | tf_op jit(solution)/shard_map/ppermute | solution.py:278
  18.9 0.1 collective-permute-start.4
  19.1 1.4 %collective-permute-done.4.refs_5_ = bf16[4,32,1024]{2,1,0:T(8,128)(2,1)S(1)} collective-permute-done((bf16[4,32,1024]{2,1,0:T(8,128)(2,1)S(1)}, bf16[4,32,1024]{2,1,0:T(8,128)(2,1)S(1)}, u32[]{:S(2)}, u32[]{:S(2)}) %collective-permute-start.4) | collective-permute-done | bytes 262176 | tf_op jit(solution)/shard_map/ppermute | solution.py:283
  20.5 3.9 %band_inner.1 = (f32[8,1,1024]{2,1,0:T(1,128)S(1)}, bf16[4,1664,128]{2,1,0:T(8,128)(2,1)S(1)}, bf16[4,128,1024]{2,1,0:T(8,128)(2,1)S(1)}) custom-call(s32[25]{0:T(128)S(1)} %pad_add_fusion.numbers, bf16[2,32,1024]{2,1,0:T(8,128)(2,1)S(1)} %get-tuple-element.30.refs_0_, bf16[2,32,1024]{2,1,0:T(8,128)(2,1)S(1)} %collective-permute-done.refs_1_, ...), custom_call_target="tpu_custom_call" | custom-call | tf_op jit(solution)/shard_map/band_inner/pallas_call | solution.py:181
  24.4 0.6 %collective-permute-done.5.rim = bf16[4,32,1024]{2,1,0:T(8,128)(2,1)S(1)} collective-permute-done((bf16[4,32,1024]{2,1,0:T(8,128)(2,1)S(1)}, bf16[4,32,1024]{2,1,0:T(8,128)(2,1)S(1)}, u32[]{:S(2)}, u32[]{:S(2)}) %collective-permute-start.5) | collective-permute-done | bytes 262176 | tf_op jit(solution)/shard_map/ppermute | solution.py:284
  25.0 2.6 %band_given.1 = (f32[2,2,2,1024]{3,2,1,0:T(2,128)S(1)}, bf16[4,1664,128]{2,1,0:T(8,128)(2,1)S(1)}, bf16[4,128,1024]{2,1,0:T(8,128)(2,1)S(1)}) custom-call(s32[25]{0:T(128)S(1)} %pad_add_fusion.numbers, bf16[4,32,1024]{2,1,0:T(8,128)(2,1)S(1)} %collective-permute-done.5.rim, ...), custom_call_target="tpu_custom_call", output_to_operand_aliasing={{1}: (3, {}), {2}: (4, {})} | custom-call | tf_op jit(solution)/shard_map/band_given/pallas_call | solution.py:224
  27.6 0.5 %collective-permute-start.6 = (f32[2,2,2,1024]{3,2,1,0:T(2,128)S(1)}, f32[2,2,2,1024]{3,2,1,0:T(2,128)S(1)}, u32[]{:S(2)}, u32[]{:S(2)}) collective-permute-start(f32[2,2,2,1024]{3,2,1,0:T(2,128)S(1)} %get-tuple-element.26), channel_id=1, source_target_pairs={{14,15},{15,14},{10,11},{11,10},{6,7},{7,6},{2,3},{3,2},{0,1},{1,0... | collective-permute-start | bytes 98312 | tf_op jit(solution)/shard_map/ppermute | solution.py:287
  28.1 1.9 %band_kept.1 = f32[2,2,2,1024]{3,2,1,0:T(2,128)S(1)} custom-call(s32[25]{0:T(128)S(1)} %pad_add_fusion.numbers, f32[8,1,1024]{2,1,0:T(1,128)S(1)} %get-tuple-element.21.done, bf16[4,1664,128]{2,1,0:T(8,128)(2,1)S(1)} %get-tuple-element.24.right, bf16[4,128,1024]{2,1,0:T(8,128)(2,1)S(1)} %get-tuple-element.25.left), custom_call_target="tpu_custom_call" | custom-call | tf_op jit(solution)/shard_map/band_kept/pallas_call | solution.py:249
  30.1 0.1 collective-permute-start.7
  30.3 2.0 %collective-permute-start.8 = (f32[2,4,1024]{2,1,0:T(4,128)S(1)}, f32[2,4,1024]{2,1,0:T(4,128)S(1)}, u32[]{:S(2)}, u32[]{:S(2)}) collective-permute-start(f32[2,4,1024]{2,1,0:T(4,128)S(1)} %get-tuple-element.40), channel_id=1, source_target_pairs={{15,2},{7,3},{11,6},{3,7},{14,10},{6,11},{10,14},{2,15},{0,4},{8,5... | collective-permute-start | bytes 98312 | tf_op jit(solution)/shard_map/ppermute | solution.py:290
  32.3 2.2 %collective-permute-done.7 = f32[2,4,1024]{2,1,0:T(4,128)S(1)} collective-permute-done((f32[2,4,1024]{2,1,0:T(4,128)S(1)}, f32[2,4,1024]{2,1,0:T(4,128)S(1)}, u32[]{:S(2)}, u32[]{:S(2)}) %collective-permute-start.7) | collective-permute-done | bytes 32800 | tf_op jit(solution)/shard_map/ppermute | solution.py:290
  34.5 1.0 %collective-permute-done.8 = f32[2,4,1024]{2,1,0:T(4,128)S(1)} collective-permute-done((f32[2,4,1024]{2,1,0:T(4,128)S(1)}, f32[2,4,1024]{2,1,0:T(4,128)S(1)}, u32[]{:S(2)}, u32[]{:S(2)}) %collective-permute-start.8) | collective-permute-done | bytes 32800 | tf_op jit(solution)/shard_map/ppermute | solution.py:290
  35.4 0.7 %maximum_select_fusion.1 = f32[2,8,1024]{2,1,0:T(8,128)} fusion(f32[2,4,1024]{2,1,0:T(4,128)S(1)} %collective-permute-done.8, f32[2,4,1024]{2,1,0:T(4,128)S(1)} %broadcast_select_fusion.2, pred[]{:T(512)S(6)} %eq.21), kind=kLoop, calls=%fused_computation.5 | loop fusion | flops 49152 | bytes 131073 | tf_op jit(solution)/shard_map/jit(_where)/select_n | solution.py:292
  (19 shorter events, 0.4 us)
Async XLA Ops:
  0.0 7.8 %copy-start = (s32[2,4]{1,0:T(2,128)S(1)}, s32[2,4]{1,0:T(2,128)}, u32[]{:S(2)}) copy-start(s32[2,4]{1,0:T(2,128)} %param.7) | copy-start | bytes 100
  0.0 7.9 %copy-start.1 = (s32[2,4]{1,0:T(2,128)S(1)}, s32[2,4]{1,0:T(2,128)}, u32[]{:S(2)}) copy-start(s32[2,4]{1,0:T(2,128)} %param.8) | copy-start | bytes 100
  0.0 8.0 %copy-start.2 = (s32[2,4]{1,0:T(2,128)S(1)}, s32[2,4]{1,0:T(2,128)}, u32[]{:S(2)}) copy-start(s32[2,4]{1,0:T(2,128)} %param.9) | copy-start | bytes 100
  2.1 7.6 %collective-permute-start.3 = (bf16[2,32,1024]{2,1,0:T(8,128)(2,1)S(1)}, bf16[2,32,1024]{2,1,0:T(8,128)(2,1)S(1)}, u32[]{:S(2)}, u32[]{:S(2)}) collective-permute-start(bf16[2,32,1024]{2,1,0:T(8,128)(2,1)S(1)} %get-tuple-element.27), channel_id=1, source_target_pairs={{2,14},{3,6},{6,10},{7,2},{10,15},{11,7},{14,11},{15,3},{4,1},{5,9... | collective-permute-start | bytes 393224 | tf_op jit(solution)/shard_map/ppermute | solution.py:278
  6.3 7.7 %collective-permute-start.2 = (bf16[2,32,1024]{2,1,0:T(8,128)(2,1)S(1)}, bf16[2,32,1024]{2,1,0:T(8,128)(2,1)S(1)}, u32[]{:S(2)}, u32[]{:S(2)}) collective-permute-start(bf16[2,32,1024]{2,1,0:T(8,128)(2,1)S(1)} %get-tuple-element.28), channel_id=1, source_target_pairs={{2,15},{3,7},{6,11},{7,3},{10,14},{11,6},{14,10},{15,2},{4,0},{5,8... | collective-permute-start | bytes 393224 | tf_op jit(solution)/shard_map/ppermute | solution.py:278
  6.9 7.1 %collective-permute-start.1 = (bf16[2,32,1024]{2,1,0:T(8,128)(2,1)S(1)}, bf16[2,32,1024]{2,1,0:T(8,128)(2,1)S(1)}, u32[]{:S(2)}, u32[]{:S(2)}) collective-permute-start(bf16[2,32,1024]{2,1,0:T(8,128)(2,1)S(1)} %get-tuple-element.29), channel_id=1, source_target_pairs={{2,10},{3,2},{6,14},{7,6},{10,11},{11,3},{14,15},{15,7},{4,5},{5,1... | collective-permute-start | bytes 393224 | tf_op jit(solution)/shard_map/ppermute | solution.py:278
  7.3 11.5 %collective-permute-start = (bf16[2,32,1024]{2,1,0:T(8,128)(2,1)S(1)}, bf16[2,32,1024]{2,1,0:T(8,128)(2,1)S(1)}, u32[]{:S(2)}, u32[]{:S(2)}) collective-permute-start(bf16[2,32,1024]{2,1,0:T(8,128)(2,1)S(1)} %get-tuple-element.30.refs_0_), channel_id=1, source_target_pairs={{2,11},{3,7},{6,15},{7,3},{10,14},{11,2},{14,10},{15,6},{4,0},{5,1... | collective-permute-start | bytes 393224 | tf_op jit(solution)/shard_map/ppermute | solution.py:278
  18.9 1.6 %collective-permute-start.4 = (bf16[4,32,1024]{2,1,0:T(8,128)(2,1)S(1)}, bf16[4,32,1024]{2,1,0:T(8,128)(2,1)S(1)}, u32[]{:S(2)}, u32[]{:S(2)}) collective-permute-start(bf16[4,32,1024]{2,1,0:T(8,128)(2,1)S(1)} %pad_maximum_fusion), channel_id=1, source_target_pairs={{14,15},{15,14},{10,11},{11,10},{6,7},{7,6},{2,3},{3,2},{0,1},{1,0... | collective-permute-start | bytes 786440 | tf_op jit(solution)/shard_map/ppermute | solution.py:283
  19.0 6.0 %collective-permute-start.5 = (bf16[4,32,1024]{2,1,0:T(8,128)(2,1)S(1)}, bf16[4,32,1024]{2,1,0:T(8,128)(2,1)S(1)}, u32[]{:S(2)}, u32[]{:S(2)}) collective-permute-start(bf16[4,32,1024]{2,1,0:T(8,128)(2,1)S(1)} %pad_maximum_fusion.1), channel_id=1, source_target_pairs={{15,10},{11,6},{7,2},{3,0},{1,4},{5,8},{9,12},{13,14},{10,15},{6,1... | collective-permute-start | bytes 786440 | tf_op jit(solution)/shard_map/ppermute | solution.py:284
  27.6 2.4 %collective-permute-start.6 = (f32[2,2,2,1024]{3,2,1,0:T(2,128)S(1)}, f32[2,2,2,1024]{3,2,1,0:T(2,128)S(1)}, u32[]{:S(2)}, u32[]{:S(2)}) collective-permute-start(f32[2,2,2,1024]{3,2,1,0:T(2,128)S(1)} %get-tuple-element.26), channel_id=1, source_target_pairs={{14,15},{15,14},{10,11},{11,10},{6,7},{7,6},{2,3},{3,2},{0,1},{1,0... | collective-permute-start | bytes 98312 | tf_op jit(solution)/shard_map/ppermute | solution.py:287
  30.1 4.3 %collective-permute-start.7 = (f32[2,4,1024]{2,1,0:T(4,128)S(1)}, f32[2,4,1024]{2,1,0:T(4,128)S(1)}, u32[]{:S(2)}, u32[]{:S(2)}) collective-permute-start(f32[2,4,1024]{2,1,0:T(4,128)S(1)} %get-tuple-element.39), channel_id=1, source_target_pairs={{11,2},{7,3},{15,6},{3,7},{14,10},{2,11},{10,14},{6,15},{0,4},{12,... | collective-permute-start | bytes 98312 | tf_op jit(solution)/shard_map/ppermute | solution.py:290
  30.3 5.2 %collective-permute-start.8 = (f32[2,4,1024]{2,1,0:T(4,128)S(1)}, f32[2,4,1024]{2,1,0:T(4,128)S(1)}, u32[]{:S(2)}, u32[]{:S(2)}) collective-permute-start(f32[2,4,1024]{2,1,0:T(4,128)S(1)} %get-tuple-element.40), channel_id=1, source_target_pairs={{15,2},{7,3},{11,6},{3,7},{14,10},{6,11},{10,14},{2,15},{0,4},{8,5... | collective-permute-start | bytes 98312 | tf_op jit(solution)/shard_map/ppermute | solution.py:290
